TPU v7x, 32 devices: a whole 2x2x4 slice. The times are simulated.
32 devices in a mesh: seq: 8 (over z, y), head: 4 (over x, core).
Axes of the slice: x: 2, y: 2, z: 4, core: 2. Of those that a mesh axis runs over, the one named last changes fastest.
Arguments:
- x_quant: bfloat16 [1024, 8192], P('seq', 'head'), may hold values from -6 to 6
- scale_exp: int32 [64, 1024], P('head', 'seq'), may hold values from -2 to 1
- dt_raw: bfloat16 [128, 1024], P('head', 'seq'), may hold values from -5 to 5
- dt_bias: float32 [128], P('head'), may hold values from -3 to -1
- a_log: float32 [128], P('head')
- skip_weight: float32 [128], P('head'), may hold values from 0.5 to 1.5
- b_proj: bfloat16 [1024, 128], P('seq'), may hold values from -4 to 4
- c_proj: bfloat16 [1024, 128], P('seq'), may hold values from -0.5 to 0.5
- doc_starts: int32 [8, 2], P('seq'), may hold values from 0 to 128, as said below
- grad_out: bfloat16 [1024, 8192], P('seq', 'head'), may hold values from -6 to 6
Outputs:
- grad_x: bfloat16 [1024, 8192], P('seq', 'head')
- grad_dt: float32 [128, 1024], P('head', 'seq')
- grad_bc: float32 [2, 1024, 128], P(None, 'seq')
- head_grads: float32 [2, 128], P(None, 'head')
Inputs may be any that keep to these rules, and one draw needn't show every extreme that they name: `doc_starts`: each entry is the offset within its slab of 128 tokens of a token that begins a document, or 128 for an unused entry; a slab's entries are in no order and may repeat.
All inputs are finite; a program needn't handle non-finite values.
Results may differ from a plain program's by a relative error of at most 0.0024.
Values sent between devices are 32-bit elements; how exact they have to be, the bound alone decides.
A program may use at most 128 MiB of HBM per device.

v0:
```python
import math

import jax
import jax.numpy as jnp
from jax import lax
from jax.sharding import PartitionSpec as P

HEAD_DIM = 64
SPAN = 256


def carried_in(part, axis, combine, identity, reverse):
    count = lax.axis_size(axis)
    place = lax.axis_index(axis)
    ahead = count - 1 - place if reverse else place
    gathered = jax.tree.map(lambda a: lax.all_gather(a, axis), part)
    state = jax.tree.map(lambda a, e: jnp.zeros_like(a) + jnp.asarray(e, a.dtype), part, identity)

    def one(lap, state):
        source = count - 1 - lap if reverse else lap
        return combine(
            state, jax.tree.map(lambda a: lax.dynamic_index_in_dim(a, source, 0, False), gathered)
        )

    return lax.fori_loop(0, ahead, one, state)


def chain_step(earlier, latter):
    return (earlier[0] * latter[0], latter[1] + latter[0][:, None, None] * earlier[1])


def local(
    x_quant, scale_exp, dt_raw, dt_bias, a_log, skip_weight, b_proj, c_proj, doc_starts, grad_out
):
    highest = lax.Precision.HIGHEST
    tokens_here = x_quant.shape[0]
    heads_here = dt_raw.shape[0]
    head_width = HEAD_DIM
    state_width = b_proj.shape[1]
    scale_blocks = scale_exp.shape[0]
    span_len = min(SPAN, tokens_here)
    block_count = tokens_here // span_len
    factor = jnp.left_shift(jnp.int32(1), scale_exp + 8).astype(jnp.float32) / 256.0
    x_vals = (
        (x_quant.astype(jnp.float32).reshape(tokens_here, scale_blocks, 128) * factor.T[:, :, None])
        .reshape(tokens_here, heads_here * head_width)
        .astype(jnp.bfloat16)
    )
    x_heads = (
        x_vals.astype(jnp.float32)
        .reshape(tokens_here, heads_here, head_width)
        .transpose(1, 0, 2)
        .reshape(heads_here, block_count, span_len, head_width)
    )
    g_heads = (
        grad_out.astype(jnp.float32)
        .reshape(tokens_here, heads_here, head_width)
        .transpose(1, 0, 2)
        .reshape(heads_here, block_count, span_len, head_width)
    )
    position = jnp.arange(tokens_here, dtype=jnp.int32)
    resets = jnp.any(position[:, None] == doc_starts[0][None, :], axis=1)
    segment = jnp.cumsum(resets.astype(jnp.int32).reshape(block_count, span_len), axis=1)
    offsets = jnp.arange(span_len, dtype=jnp.int32)
    same_doc = (offsets[:, None] >= offsets[None, :])[None] & (
        segment[:, :, None] == segment[:, None, :]
    )
    pre_act = dt_raw.astype(jnp.float32) + dt_bias[:, None]
    step_size = jax.nn.softplus(pre_act)
    decay_rate = jnp.exp(a_log)
    step_blocks = step_size.reshape(heads_here, block_count, span_len)
    cumulative = jnp.cumsum(-decay_rate[:, None, None] * step_blocks, axis=2)
    first_doc = (segment == 0).astype(jnp.float32)
    last_doc = (segment == segment[:, -1:]).astype(jnp.float32)
    enter_decay = jnp.exp(cumulative) * first_doc[None]
    exit_decay = jnp.exp(cumulative[:, :, -1:] - cumulative) * last_doc[None]
    block_decay = jnp.exp(cumulative[:, :, -1]) * first_doc[None, :, -1]
    b_blocks = b_proj.astype(jnp.float32).reshape(block_count, span_len, state_width)
    c_blocks = c_proj.astype(jnp.float32).reshape(block_count, span_len, state_width)
    scaled_input = x_heads * step_blocks[:, :, :, None]
    kernel = jnp.einsum(
        "qtn,qsn->qts",
        c_proj.reshape(block_count, span_len, state_width),
        b_proj.reshape(block_count, span_len, state_width),
        preferred_element_type=jnp.float32,
    )
    block_state = jnp.einsum(
        "hqsp,qsn->hqpn", exit_decay[:, :, :, None] * scaled_input, b_blocks, precision=highest
    )
    block_grad = jnp.einsum(
        "hqtp,qtn->hqpn", enter_decay[:, :, :, None] * g_heads, c_blocks, precision=highest
    )
    local_state = block_state[:, 0]
    slab_decay = block_decay[:, 0]
    local_grad = block_grad[:, block_count - 1]
    identity = (jnp.ones_like(slab_decay), jnp.zeros_like(local_state))
    state_entry = carried_in((slab_decay, local_state), "seq", chain_step, identity, False)[1]
    grad_exit = carried_in((slab_decay, local_grad), "seq", chain_step, identity, True)[1]
    carried = state_entry
    number = 0
    entries = [carried]
    carried = block_decay[:, number][:, None, None] * carried + block_state[:, number]
    exits = [carried] * block_count
    carried = grad_exit
    number = 0
    exits[number] = carried
    entry_states = jnp.stack(entries, 1)
    exit_grads = jnp.stack(exits, 1)
    group_size = math.gcd(heads_here, max(1, (1 << 21) // (span_len * span_len)))
    group_count = heads_here // group_size
    number = 0

    def within_block(groups, doc_mask=same_doc[number], kern=kernel[number]):
        cumul_group, inputs_group, grads_group = groups
        log_gap = cumul_group[:, :, None] - cumul_group[:, None, :]
        decay_mat = jnp.exp(jnp.where(doc_mask[None], log_gap, -1e30))
        weighted = decay_mat * kern[None]
        input_grad = jnp.einsum("hts,htp->hsp", weighted, grads_group, precision=highest)
        scores = jnp.einsum("htp,hsp->hts", grads_group, inputs_group, precision=highest)
        kernel_part = decay_mat * scores
        flow_terms = kernel_part * kern[None]
        return (
            input_grad,
            jnp.sum(kernel_part, 0),
            jnp.sum(flow_terms, 2) - jnp.sum(flow_terms, 1),
        )

    input_grad, kernel_grad, cumul_grad = lax.map(
        within_block,
        (
            cumulative[:, number].reshape(group_count, group_size, span_len),
            scaled_input[:, number].reshape(group_count, group_size, span_len, head_width),
            g_heads[:, number].reshape(group_count, group_size, span_len, head_width),
        ),
    )
    input_parts = [input_grad.reshape(heads_here, span_len, head_width)]
    kernel_parts = [jnp.sum(kernel_grad, 0)]
    cumul_parts = [cumul_grad.reshape(heads_here, span_len)]
    inner_grad = jnp.stack(input_parts, 1)
    kernel_grad = jnp.stack(kernel_parts, 0)
    cumul_grad = jnp.stack(cumul_parts, 1)
    state_read = jnp.einsum("hqpn,qtn->hqtp", entry_states, c_blocks, precision=highest)
    enter_grad = jnp.sum(g_heads * state_read, axis=3)
    c_extra = jnp.einsum(
        "hqtp,hqpn->qtn", enter_decay[:, :, :, None] * g_heads, entry_states, precision=highest
    )
    back_proj = jnp.einsum("hqpn,qsn->hqsp", exit_grads, b_blocks, precision=highest)
    input_total = inner_grad + exit_decay[:, :, :, None] * back_proj
    exit_grad = jnp.sum(scaled_input * back_proj, axis=3)
    b_extra = jnp.einsum(
        "hqsp,hqpn->qsn", exit_decay[:, :, :, None] * scaled_input, exit_grads, precision=highest
    )
    block_scalar = jnp.sum(exit_grads * entry_states, axis=(2, 3))
    grad_b = (
        jnp.einsum("qts,qtn->qsn", kernel_grad, c_blocks, precision=highest) + b_extra
    ).reshape(tokens_here, state_width)
    grad_c = (
        jnp.einsum("qts,qsn->qtn", kernel_grad, b_blocks, precision=highest) + c_extra
    ).reshape(tokens_here, state_width)
    cumul_total = cumul_grad + enter_grad * enter_decay - exit_grad * exit_decay
    last_terms = jnp.sum(exit_grad * exit_decay, axis=2) + block_scalar * block_decay
    cumul_total = cumul_total.at[:, :, -1].add(last_terms)
    decay_grad = jnp.flip(jnp.cumsum(jnp.flip(cumul_total, 2), 2), 2).reshape(
        heads_here, tokens_here
    )
    step_grad = (
        jnp.sum(input_total * x_heads, axis=3).reshape(heads_here, tokens_here)
        - decay_rate[:, None] * decay_grad
    )
    grad_dt = step_grad * jax.nn.sigmoid(pre_act)
    alog_part = -jnp.sum(decay_grad * step_size, axis=1) * decay_rate
    skip_part = jnp.sum(g_heads * x_heads, axis=(1, 2, 3))
    grad_heads = (
        input_total * step_blocks[:, :, :, None] + skip_weight[:, None, None, None] * g_heads
    )
    grad_x = (
        grad_heads.reshape(heads_here, tokens_here, head_width)
        .transpose(1, 0, 2)
        .reshape(tokens_here, heads_here * head_width)
        .astype(jnp.bfloat16)
    )
    grad_bc = lax.psum(jnp.stack([grad_b, grad_c]), "head")
    totals = lax.psum(jnp.stack([alog_part, skip_part]), "seq")
    total_tokens = tokens_here * lax.axis_size("seq")
    head_grads = totals / math.sqrt(total_tokens * head_width)
    return (grad_x, grad_dt, grad_bc, head_grads)


def solution(mesh):
    in_specs = (
        P("seq", "head"),
        P("head", "seq"),
        P("head", "seq"),
        P("head"),
        P("head"),
        P("head"),
        P("seq", None),
        P("seq", None),
        P("seq", None),
        P("seq", "head"),
    )
    out_specs = (P("seq", "head"), P("head", "seq"), P(None, "seq", None), P(None, "head"))
    return jax.shard_map(local, mesh=mesh, in_specs=in_specs, out_specs=out_specs, check_vma=False)
```

profile of v0, /device:TPU:0, one launch (start us, length us, event | category | flops | bytes accessed | tf_op | source)
XLA Modules:
  0.0 351.6 jit_solution(7842547482789941245)
XLA Ops:
  7.2 0.7 compare_reduce_fusion
  8.0 0.3 reduce_window_sum.29
  8.3 0.6 slice.34
  8.9 0.6 compare_convert_fusion.1
  9.5 0.7 fusion.50
  10.2 1.3 copy.41
  11.5 0.8 compare_select_fusion
  12.4 0.3 reduce_window_sum.30
  12.7 2.5 convolution_bitcast_fusion.3
  15.3 0.6 slice.35
  16.5 0.6 dynamic-slice.10
  17.7 0.2 slice_reduce_fusion
  17.9 0.2 dynamic-update-slice.3
  18.2 23.6 %all-reduce = f32[256]{0:T(256)S(1)} all-reduce(f32[256]{0:T(256)S(1)} %dynamic-update-slice.3), channel_id=3, replica_groups=mesh['seq'=8,'head'=4] {'seq'}, use_global_device_ids=true, to_apply=%add | all-reduce | flops 256 | bytes 2048
  42.0 0.3 mul.322
  42.4 0.4 fusion.30
  42.8 0.3 copy.45
  43.1 100.4 %all-gather.6.cloned.1.call-done = f32[256,1,64,128]{3,2,1,0:T(8,128)} async-done(((f32[32,1,64,128]{3,2,1,0:T(8,128)}), f32[256,1,64,128]{3,2,1,0:T(8,128)}) %all-gather.6.cloned.1.call-update) | async-done | bytes 8388624 | tf_op jit(solution)/shard_map/all_gather | solution.py:16
  143.6 10.4 %while.33 = (s32[]{:T(128)}, f32[32,64,128]{2,1,0:T(8,128)S(1)}, s32[]{:T(128)}, f32[8,32,64,128]{3,2,1,0:T(8,128)}, f32[8,32]{1,0:T(8,128)S(1)}, /*index=5*/s32[]{:T(128)}, s32[]{:T(128)}, s32[]{:T(128)}, s32[]{:T(128)}) while((s32[]{:T(128)}, f32[32,64,128]{2,1,0:T(8,128)S(1)}, s32[]{:T(128)}, f32[8,32,64,128]{3,2,1,0:T(8,128)}, ...), condition=%wide.region_4.5_spmd, body=%wide.region_3.4_spmd.sunk | while | flops 524294 | bytes 3146267 | solution.py:25
  143.7 1.4 bitcast_add_fusion.4
  145.2 1.4 bitcast_add_fusion.4
  146.7 1.4 bitcast_add_fusion.4
  148.2 1.4 bitcast_add_fusion.4
  149.6 1.4 bitcast_add_fusion.4
  151.1 1.4 bitcast_add_fusion.4
  152.6 1.4 bitcast_add_fusion.4
  154.1 1.7 fusion.19
  155.8 0.2 multiply_reduce_fusion.4
  156.0 1.6 convolution_bitcast_fusion.1
  157.7 0.3 fusion.17
  158.3 3.1 multiply_reduce_fusion
  161.4 2.6 multiply_reduce_fusion.3
  164.0 1.0 copy.49
  165.1 1.8 convolution_bitcast_fusion.4
  167.1 112.9 %all-gather.8.cloned.1.call-done = f32[256,1,64,128]{3,2,1,0:T(8,128)} async-done(((f32[32,1,64,128]{3,2,1,0:T(8,128)}), f32[256,1,64,128]{3,2,1,0:T(8,128)}) %all-gather.8.cloned.1.call-update) | async-done | bytes 8388624 | tf_op jit(solution)/shard_map/all_gather | solution.py:16
  280.1 0.2 while.34
  280.3 0.3 multiply_reduce_fusion.2
  280.6 0.6 fusion.10
  281.3 1.8 fusion.11
  283.2 0.2 fusion.12
  283.6 0.2 scatter-add.4
  283.9 0.3 reduce_window_sum.31
  284.2 0.8 fusion.45
  285.1 28.8 %psum.15 = f32[2,32]{1,0:T(2,128)S(1)} all-reduce(f32[2,32]{1,0:T(2,128)S(1)} %pad_maximum_fusion.1), channel_id=1, replica_groups=mesh['seq'=8,'head'=4] {'seq'}, use_global_device_ids=true, to_apply=%region_19.20 | all-reduce | flops 64 | bytes 512 | tf_op jit(solution)/shard_map/psum | solution.py:183
  313.9 0.7 pad_maximum_fusion
  314.6 0.6 broadcast_multiply_fusion
  315.2 28.3 %all-reduce.3.cloned.1.call-done = f32[2,128,128]{2,1,0:T(8,128)} async-done(((f32[2,128,128]{2,1,0:T(8,128)}), f32[2,128,128]{2,1,0:T(8,128)}) %all-reduce.3.cloned.1.call-update) | async-done | bytes 131088 | tf_op jit(solution)/shard_map/psum | solution.py:182
  343.5 1.6 copy.73
  (53 shorter events, 1.6 us)
Async XLA Ops:
  7.2 146.9 %copy-start = (bf16[128,128]{1,0:T(8,128)(2,1)S(1)}, bf16[128,128]{1,0:T(8,128)(2,1)}, u32[]{:S(2)}) copy-start(bf16[128,128]{1,0:T(8,128)(2,1)} %param.22) | copy-start | bytes 98308
  7.2 9.3 %copy-start.9 = (u32[32]{0:T(128)S(1)}, u32[32]{0:T(128)}, u32[]{:S(2)}) copy-start(u32[32]{0:T(128)} %constant.139) | copy-start | bytes 388
  7.2 34.7 %copy-start.5 = (s32[16,128]{1,0:T(8,128)S(1)}, s32[16,128]{1,0:T(8,128)}, u32[]{:S(2)}) copy-start(s32[16,128]{1,0:T(8,128)} %param.17) | copy-start | bytes 24580
  7.2 136.3 %all-gather.6.cloned.1.call-start = ((), (), s32[]{:S(2)}) async-start(), calls=%async_computation.1 | async-start | bytes 9437184 | tf_op jit(solution)/shard_map/all_gather | solution.py:16
  11.5 30.8 %copy-start.2 = (bf16[128,2048]{1,0:T(8,128)(2,1)S(1)}, bf16[128,2048]{1,0:T(8,128)(2,1)}, u32[]{:S(2)}) copy-start(bf16[128,2048]{1,0:T(8,128)(2,1)} %param.16) | copy-start | bytes 1572868
  15.2 264.8 %all-gather.8.cloned.1.call-start = ((), (), s32[]{:S(2)}) async-start(), calls=%async_computation.2 | async-start | bytes 9437184 | tf_op jit(solution)/shard_map/all_gather | solution.py:16
  156.0 2.1 copy-start.3
  157.6 185.8 %all-reduce.3.cloned.1.call-start = ((), (), s32[]{:S(2)}) async-start(), calls=%async_computation | async-start | bytes 262144 | tf_op jit(solution)/shard_map/psum | solution.py:182
  158.3 3.1 copy-start.1
  158.3 3.1 copy-start.7
  280.6 3.6 %copy-start.4 = (bf16[32,128]{1,0:T(8,128)(2,1)S(1)}, bf16[32,128]{1,0:T(8,128)(2,1)}, u32[]{:S(2)}) copy-start(bf16[32,128]{1,0:T(8,128)(2,1)} %param.18) | copy-start | bytes 24580
  280.6 3.6 %copy-start.6 = (f32[32]{0:T(128)S(1)}, f32[32]{0:T(128)}, u32[]{:S(2)}) copy-start(f32[32]{0:T(128)} %param.19) | copy-start | bytes 388
  280.6 4.4 %copy-start.8 = (f32[32]{0:T(128)S(1)}, f32[32]{0:T(128)}, u32[]{:S(2)}) copy-start(f32[32]{0:T(128)} %param.20) | copy-start | bytes 388
Sparse Core Ops, SparseCore 0:
  15.3 128.1 all-gather.5
  157.8 122.1 all-gather.7
  314.7 28.6 all-reduce.2
where the time goes:
time: 352 us
  waiting for transfers between devices  242 us (69%)
  blocking collectives  52.5 us (15%)
  other arithmetic  17.7 us (5%)
  matrix products  16.3 us (5%)
  between operations  15.4 us (4%)
  local copies, waits for them, and re-layouts  7.56 us (2%)
    all_gather x2, waiting for transfers between devices, carried_in(): gathered = jax.tree.map(lambda a: lax.all_gather(a, axis), part)  213 us
    psum x1, blocking collectives, local(): totals = lax.psum(jnp.stack([alog_part, skip_part]), 'seq')  28.8 us
    psum x1, waiting for transfers between devices, local(): grad_bc = lax.psum(jnp.stack([grad_b, grad_c]), 'head')  28.3 us
    unnamed x1, blocking collectives  23.6 us
    add x7, other arithmetic, chain_step(): latter[1] + latter[0][:, None, None] * earlier[1]  10.1 us
  transfers between devices with their start and end apart: 3, of which 3 were waited for; matrix products, arithmetic and copies ran while one was open for 4% of the time, Pallas kernels for 0%

commit v1 on v0

v1 whole, which is shorter than its diff:
```python
import functools
import math

import jax
import jax.numpy as jnp
from jax import lax
from jax.experimental import pallas as pl
from jax.experimental.pallas import tpu as pltpu
from jax.sharding import PartitionSpec as P

HEAD_DIM = 64
MESH = pl.DeviceIdType.MESH
F32 = jnp.float32
BF16 = jnp.bfloat16
HIGHEST = lax.Precision.HIGHEST

ROWS = ((1,), (1,))
COLS = ((0,), (0,))
PLAIN = ((1,), (0,))


def mm(a, b, dims):
    return lax.dot_general(a, b, (dims, ((), ())), preferred_element_type=F32)


def split(a):
    high = a.astype(BF16)
    return high, (a - high.astype(F32)).astype(BF16)


def mm2(a, b, dims):
    high, low = split(a)
    return mm(high, b, dims) + mm(low, b, dims)


def mm2r(a, b, dims):
    high, low = split(b)
    return mm(a, high, dims) + mm(a, low, dims)


def mm3(a, b, dims):
    a_high, a_low = split(a)
    b_high, b_low = split(b)
    return mm(a_high, b_high, dims) + (mm(a_high, b_low, dims) + mm(a_low, b_high, dims))


def kernel(
    nseq, nhead, norm,
    x_ref, sc_ref, dt_ref, bias_ref, alog_ref, skip_ref, b_ref, c_ref, doc_ref, g_ref,
    gx_out, dt_out, bc_out, hg_out,
    fac, steps, cums, rates, sigm, skips, meta, msend, bcf, xgs, xg, kern, same, first, last,
    xs_s, ge_s, exit_s, loc, es, rs_, er, rr, gxa, gxr, kg, cx, skp, ct, sg, sgr, bcp, red, gat, hgp,
    meta_sems, bc_sems, xg_send, xg_recv, e_send, e_recv, r_send, r_recv, gx_send, gx_recv,
    sg_sems, red_send, red_recv, gat_send, gat_recv, hg_send, hg_recv,
):
    me, hd = lax.axis_index("seq"), lax.axis_index("head")
    par, z = lax.rem(me, 2), lax.div(me, 2)
    zs = nseq // 2
    oth = 1 - par
    partner = me + 1 - 2 * par
    tok = x_ref.shape[0]
    heads = dt_ref.shape[0]
    half = heads // 2
    npair = half // 2

    barrier = pltpu.get_barrier_semaphore()
    for j in range(1, nseq):
        pl.semaphore_signal(barrier, inc=1, device_id=(lax.rem(me + j, nseq), hd), device_id_type=MESH)
    for j in range(1, nhead):
        there = lax.rem(hd + j, nhead)
        pl.semaphore_signal(barrier, inc=1, device_id=(me, there), device_id_type=MESH)
        pl.semaphore_signal(barrier, inc=1, device_id=(partner, there), device_id_type=MESH)

    def remote(src, dst, send, recv, device):
        return pltpu.make_async_remote_copy(
            src_ref=src, dst_ref=dst, send_sem=send, recv_sem=recv,
            device_id=device, device_id_type=MESH,
        )

    across = (partner, hd)

    def bc_copy(slab):
        return remote(bcf.at[slab], bcf.at[slab], bc_sems.at[0], bc_sems.at[1], across)

    def meta_copy(slab):
        return remote(msend, meta.at[slab], meta_sems.at[0], meta_sems.at[1], across)

    def xg_copy(slab, k):
        return remote(xgs.at[k], xg.at[slab, k], xg_send.at[k], xg_recv.at[k], across)

    def e_copy(k):
        return remote(es.at[k], er.at[k], e_send.at[k], e_recv.at[k], (lax.rem(me + 2, nseq), hd))

    def r_copy(k):
        return remote(rs_.at[k], rr.at[k], r_send.at[k], r_recv.at[k], (lax.rem(me + nseq - 2, nseq), hd))

    def gx_copy(k):
        return remote(gxa.at[oth, k], gxr.at[k], gx_send.at[k], gx_recv.at[k], across)

    bcf[par, 0] = b_ref[...].astype(F32)
    bcf[par, 1] = c_ref[...].astype(F32)
    fac[...] = jnp.left_shift(jnp.int32(1), sc_ref[...] + 8).astype(F32) / 256.0

    sub = lax.broadcasted_iota(jnp.int32, (heads, heads), 0)
    lane = lax.broadcasted_iota(jnp.int32, (heads, heads), 1)

    def column(ref):
        return jnp.sum(jnp.where(sub == lane, ref[...], 0.0), axis=1, keepdims=True)

    t_sub = lax.broadcasted_iota(jnp.int32, (tok, tok), 0)
    t_lane = lax.broadcasted_iota(jnp.int32, (tok, tok), 1)
    pre = dt_ref[...].astype(F32) + column(bias_ref)
    step_all = jnp.maximum(pre, 0.0) + jnp.log1p(jnp.exp(-jnp.abs(pre)))
    rate = jnp.exp(column(alog_ref))
    upper = (t_sub <= t_lane).astype(F32)
    steps[...] = step_all
    cums[...] = lax.dot_general(
        -rate * step_all, upper, (PLAIN, ((), ())), precision=HIGHEST, preferred_element_type=F32
    )
    rates[...] = jnp.broadcast_to(rate, (heads, tok))
    sigm[...] = 1.0 / (1.0 + jnp.exp(-pre))
    skips[...] = jnp.broadcast_to(column(skip_ref), (heads, tok))
    row_id = lax.broadcasted_iota(jnp.int32, (8, tok), 1)
    count = jnp.zeros((8, tok), F32)
    for j in range(doc_ref.shape[1]):
        count = count + (row_id >= doc_ref[0, j]).astype(F32)
    mine = pl.ds(pl.multiple_of(par * half, half), half)
    theirs = pl.ds(pl.multiple_of(oth * half, half), half)
    meta[par, 0:half] = steps[mine]
    meta[par, half:2 * half] = cums[mine]
    meta[par, 2 * half:2 * half + 8] = count
    msend[0:half] = steps[theirs]
    msend[half:2 * half] = cums[theirs]
    msend[2 * half:2 * half + 8] = count

    pl.semaphore_wait(barrier, nseq - 1 + 2 * (nhead - 1))
    bc_copy(par).start()
    meta_copy(par).start()

    def scaled(j):
        lanes = pl.ds(pl.multiple_of(j * tok, tok), tok)
        factor = jnp.broadcast_to(fac[pl.ds(j, 1), :], (tok, tok)).T
        return x_ref[:, lanes].astype(F32) * factor, g_ref[:, lanes].astype(F32)

    def send_pair(k, carry):
        x_val, g_val = scaled(oth * npair + k)
        xgs[k, 0] = x_val
        xgs[k, 1] = g_val
        xg_copy(par, k).start()
        return carry

    lax.fori_loop(0, npair, send_pair, 0)

    def own_pair(k, carry):
        x_val, g_val = scaled(par * npair + k)
        xg[par, k, 0] = x_val
        xg[par, k, 1] = g_val
        return carry

    lax.fori_loop(0, npair, own_pair, 0)
    kg[...] = jnp.zeros_like(kg)
    cx[...] = jnp.zeros_like(cx)

    @pl.when(z == 0)
    def _():
        er[...] = jnp.zeros_like(er)

    @pl.when(z == zs - 1)
    def _():
        rr[...] = jnp.zeros_like(rr)

    bc_copy(oth).wait_recv()
    meta_copy(oth).wait_recv()

    def pair_of(q, row):
        return meta[q, pl.ds(row, 1), :]

    for q in range(2):
        seg_row = jnp.broadcast_to(meta[q, 2 * half:2 * half + 1, :], (tok, tok))
        seg_col = seg_row.T
        end = meta[q, 2 * half:2 * half + 1, tok - 1:tok]
        same[q] = ((t_sub >= t_lane) & (seg_row == seg_col)).astype(F32)
        first[q] = (seg_col == 0.0).astype(F32)
        last[q] = (seg_col == end).astype(F32)
        kern[q] = mm(bcf[q, 1].astype(BF16), bcf[q, 0].astype(BF16), ROWS)

    def lanes_of(a, b):
        return jnp.concatenate(
            [jnp.broadcast_to(a, (HEAD_DIM, tok)), jnp.broadcast_to(b, (HEAD_DIM, tok))], axis=0
        ).T

    def slab_decay(q, k):
        whole = 1.0 - jnp.minimum(meta[q, 2 * half:2 * half + 1, tok - 1:tok], 1.0)
        ends = [
            jnp.broadcast_to(
                jnp.exp(pair_of(q, half + 2 * k + s)[:, tok - 1:tok]) * whole, (HEAD_DIM, tok)
            )
            for s in range(2)
        ]
        return jnp.concatenate(ends, axis=0)

    def local_part(k):
        xg_copy(oth, k).wait_recv()
        states, grads = [], []
        for q in range(2):
            cum = lanes_of(pair_of(q, half + 2 * k), pair_of(q, half + 2 * k + 1))
            step = lanes_of(pair_of(q, 2 * k), pair_of(q, 2 * k + 1))
            enter_w = jnp.exp(cum) * first[q]
            exit_w = jnp.exp(cum[tok - 1:tok, :] - cum) * last[q]
            xs = exit_w * (step * xg[q, k, 0])
            ge = enter_w * xg[q, k, 1]
            xs_s[k, q] = xs
            ge_s[k, q] = ge
            exit_s[k, q] = exit_w
            states.append(mm2(xs, bcf[q, 0].astype(BF16), COLS))
            grads.append(mm2(ge, bcf[q, 1].astype(BF16), COLS))
        d0, d1 = slab_decay(0, k), slab_decay(1, k)
        loc[k, 0] = d1 * states[0] + states[1]
        loc[k, 1] = d0 * grads[1] + grads[0]
        loc[k, 2] = states[0]
        loc[k, 3] = grads[1]

    def forward_part(k):
        @pl.when(z > 0)
        def _():
            e_copy(k).wait_recv()

        @pl.when(z < zs - 1)
        def _():
            es[k] = slab_decay(0, k) * slab_decay(1, k) * er[k] + loc[k, 0]
            e_copy(k).start()

    def backward_part(k):
        @pl.when(z < zs - 1)
        def _():
            r_copy(k).wait_recv()

        @pl.when(z > 0)
        def _():
            rs_[k] = slab_decay(0, k) * slab_decay(1, k) * rr[k] + loc[k, 1]
            r_copy(k).start()

    lane_a = t_lane < HEAD_DIM

    def final_part(k):
        entry0, exit1 = er[k], rr[k]
        decays = [slab_decay(0, k), slab_decay(1, k)]
        entries = [entry0, decays[0] * entry0 + loc[k, 2]]
        exits = [decays[1] * exit1 + loc[k, 3], exit1]
        skip_rows = [skips[pl.ds(par * half + 2 * k + s, 1), :] for s in range(2)]
        skip_lanes = jnp.where(lane_a[0:1], skip_rows[0], skip_rows[1])
        skip_sum = jnp.zeros((1, tok), F32)
        for q in range(2):
            x_val, g_val = xg[q, k, 0], xg[q, k, 1]
            bq, cq = bcf[q, 0].astype(BF16), bcf[q, 1].astype(BF16)
            xs, ge, exit_w = xs_s[k, q], ge_s[k, q], exit_s[k, q]
            entry, leave = entries[q], exits[q]
            read = mm2r(cq, entry, ROWS)
            back = mm2r(bq, leave, ROWS)
            cx[q, 1] += mm3(ge, entry, PLAIN)
            cx[q, 0] += mm3(xs, leave, PLAIN)
            exit_terms = xs * back
            g_two = jnp.concatenate(
                [jnp.where(lane_a, g_val, 0.0), jnp.where(lane_a, 0.0, g_val)], axis=0
            ).astype(BF16)
            scores = mm(g_two, x_val.astype(BF16), ROWS)
            weights, flows = [], []
            kern_q, mask = kern[q], same[q] > 0.5
            total = jnp.zeros((tok, tok), F32)
            for s in range(2):
                step_row = pair_of(q, 2 * k + s)
                row = jnp.broadcast_to(pair_of(q, half + 2 * k + s), (tok, tok))
                decay = jnp.exp(jnp.where(mask, row.T - row, -1e30))
                part = decay * (scores[s * tok:(s + 1) * tok] * step_row)
                total = total + part
                weights.append(decay * kern_q)
                flows.append(part * kern_q)
            kg[q] += total
            inner = mm2(jnp.concatenate(weights, axis=0), g_two, COLS)
            input_total = inner + exit_w * back
            sums = (ge * read - exit_terms).T
            moved = (input_total * x_val).T
            exit_sum = jnp.sum(exit_terms, axis=0, keepdims=True)
            both = leave * entry * decays[q]
            at_end = t_lane[0:1] == tok - 1
            for s in range(2):
                span = slice(s * HEAD_DIM, (s + 1) * HEAD_DIM)
                ending = jnp.sum(exit_sum[:, span], keepdims=True) + jnp.sum(both[span], keepdims=True)
                cumul = (
                    jnp.sum(flows[s].T - flows[s], axis=0, keepdims=True)
                    + jnp.sum(sums[span], axis=0, keepdims=True)
                    + jnp.where(at_end, ending, 0.0)
                )
                ct[q, pl.ds(2 * k + s, 1), :] = cumul
                sg[q, pl.ds(2 * k + s, 1), :] = jnp.sum(moved[span], axis=0, keepdims=True)
            skip_sum = skip_sum + jnp.sum(g_val * x_val, axis=0, keepdims=True)
            step = lanes_of(pair_of(q, 2 * k), pair_of(q, 2 * k + 1))
            gxa[q, k] = input_total * step + skip_lanes * g_val
        skp[pl.ds(k, 1), :] = skip_sum
        gx_copy(k).start()
        own_lanes = pl.ds(pl.multiple_of((par * npair + k) * tok, tok), tok)
        gx_out[:, own_lanes] = gxa[par, k].astype(BF16)

    def lap(i, carry):
        @pl.when(i < npair)
        def _():
            local_part(i)

        ahead = i - z

        @pl.when((ahead >= 0) & (ahead < npair))
        def _():
            forward_part(ahead)

        behind = i - (zs - 1 - z)

        @pl.when((behind >= 0) & (behind < npair))
        def _():
            backward_part(behind)

        @pl.when(i >= zs - 1)
        def _():
            final_part(i - (zs - 1))

        return carry

    lax.fori_loop(0, npair + zs - 1, lap, 0)

    for q in range(2):
        bcp[q, 0:tok] = mm2(kg[q], bcf[q, 1].astype(BF16), COLS) + cx[q, 0]
        bcp[q, tok:2 * tok] = mm2(kg[q], bcf[q, 0].astype(BF16), PLAIN) + cx[q, 1]
    piece = 2 * tok // nhead
    here = par * nhead + hd
    base = me - par

    def red_copy(to, slot):
        rows = pl.ds(pl.multiple_of(lax.rem(to, nhead) * piece, piece), piece)
        return remote(
            bcp.at[lax.div(to, nhead), rows], red.at[slot], red_send.at[to], red_recv.at[slot],
            (base + lax.div(to, nhead), lax.rem(to, nhead)),
        )

    for j in range(1, 2 * nhead):
        red_copy(lax.rem(here + j, 2 * nhead), here).start()

    lower = (t_sub >= t_lane).astype(F32)
    rate_own = rates[mine]
    alog_sum = jnp.zeros((half, 1), F32)
    for q in range(2):
        decay_grad = lax.dot_general(
            ct[q], lower, (PLAIN, ((), ())), precision=HIGHEST, preferred_element_type=F32
        )
        sg[q] = sg[q] - rate_own * decay_grad
        alog_sum = alog_sum - jnp.sum(decay_grad * meta[q, 0:half] * rate_own, axis=1, keepdims=True)
    sg_copy = remote(sg.at[oth], sgr, sg_sems.at[0], sg_sems.at[1], across)
    sg_copy.start()
    h_sub = lax.broadcasted_iota(jnp.int32, (half, tok), 0)
    h_lane = lax.broadcasted_iota(jnp.int32, (half, tok), 1) - par * half
    alog_row = jnp.sum(jnp.where(h_sub == h_lane, alog_sum, 0.0), axis=0, keepdims=True)
    skip_all = skp[...]
    skip_a = jnp.sum(skip_all[:, 0:HEAD_DIM], axis=1, keepdims=True)
    skip_b = jnp.sum(skip_all[:, HEAD_DIM:], axis=1, keepdims=True)
    k_sub, k_lane = 2 * h_sub[0:npair], h_lane[0:npair]
    skip_row = jnp.sum(
        jnp.where(k_sub == k_lane, skip_a, 0.0) + jnp.where(k_sub + 1 == k_lane, skip_b, 0.0),
        axis=0, keepdims=True,
    )
    r_sub = lax.broadcasted_iota(jnp.int32, (8, tok), 0)
    hgp[me] = jnp.where(r_sub == 0, alog_row, jnp.where(r_sub == 1, skip_row, 0.0))

    def hg_copy(to, slot):
        return remote(hgp.at[slot], hgp.at[slot], hg_send.at[to], hg_recv.at[slot], (to, hd))

    for j in range(1, nseq):
        hg_copy(lax.rem(me + j, nseq), me).start()

    red[here] = bcp[par, pl.ds(pl.multiple_of(hd * piece, piece), piece), :]
    for j in range(1, 2 * nhead):
        other = lax.rem(here + j, 2 * nhead)
        red_copy(other, other).wait_recv()
    gat[hd] = jnp.sum(red[...], axis=0)

    def gat_copy(to, slot):
        return remote(gat.at[slot], gat.at[slot], gat_send.at[to], gat_recv.at[slot], (me, to))

    for j in range(1, nhead):
        gat_copy(lax.rem(hd + j, nhead), hd).start()

    def take_pair(k, carry):
        gx_copy(k).wait_recv()
        lanes = pl.ds(pl.multiple_of((oth * npair + k) * tok, tok), tok)
        gx_out[:, lanes] = gxr[k].astype(BF16)
        return carry

    lax.fori_loop(0, npair, take_pair, 0)
    dt_out[mine] = sg[par] * sigm[mine]
    sg_copy.wait_recv()
    dt_out[theirs] = sgr[...] * sigm[theirs]
    for j in range(1, nseq):
        other = lax.rem(me + j, nseq)
        hg_copy(other, other).wait_recv()
    hg_out[...] = jnp.sum(hgp[...], axis=0)[0:2, 0:heads] * norm
    for j in range(1, nhead):
        other = lax.rem(hd + j, nhead)
        gat_copy(other, other).wait_recv()
    bc_out[...] = gat[...].reshape(2, tok, b_ref.shape[1])

    bc_copy(par).wait_send()
    meta_copy(par).wait_send()
    sg_copy.wait_send()

    def drain(k, carry):
        xg_copy(par, k).wait_send()
        gx_copy(k).wait_send()

        @pl.when(z < zs - 1)
        def _():
            e_copy(k).wait_send()

        @pl.when(z > 0)
        def _():
            r_copy(k).wait_send()

        return carry

    lax.fori_loop(0, npair, drain, 0)
    for j in range(1, 2 * nhead):
        red_copy(lax.rem(here + j, 2 * nhead), here).wait_send()
    for j in range(1, nhead):
        gat_copy(lax.rem(hd + j, nhead), hd).wait_send()
    for j in range(1, nseq):
        hg_copy(lax.rem(me + j, nseq), me).wait_send()


def local(
    x_quant, scale_exp, dt_raw, dt_bias, a_log, skip_weight, b_proj, c_proj, doc_starts, grad_out
):
    nseq, nhead = lax.axis_size("seq"), lax.axis_size("head")
    tok, channels = x_quant.shape
    heads = dt_raw.shape[0]
    state = b_proj.shape[1]
    half, npair = heads // 2, heads // 4
    norm = 1.0 / math.sqrt(tok * nseq * HEAD_DIM)
    vmem = lambda *shape: pltpu.VMEM(shape, F32)
    dma = lambda n: pltpu.SemaphoreType.DMA((n,))
    sq = (tok, state)
    scratch = [
        vmem(scale_exp.shape[0], tok),
        vmem(heads, tok), vmem(heads, tok), vmem(heads, tok), vmem(heads, tok), vmem(heads, tok),
        vmem(2, 2 * half + 8, tok), vmem(2 * half + 8, tok),
        vmem(2, 2, *sq),
        vmem(npair, 2, *sq), vmem(2, npair, 2, *sq),
        vmem(2, *sq), vmem(2, *sq), vmem(2, *sq), vmem(2, *sq),
        vmem(npair, 2, *sq), vmem(npair, 2, *sq), vmem(npair, 2, *sq),
        vmem(npair, 4, *sq),
        vmem(npair, *sq), vmem(npair, *sq), vmem(npair, *sq), vmem(npair, *sq),
        vmem(2, npair, *sq), vmem(npair, *sq),
        vmem(2, *sq), vmem(2, 2, *sq),
        vmem(npair, tok),
        vmem(2, half, tok), vmem(2, half, tok), vmem(half, tok),
        vmem(2, 2 * tok, state),
        vmem(2 * nhead, 2 * tok // nhead, state),
        vmem(nhead, 2 * tok // nhead, state),
        vmem(nseq, 8, tok),
        dma(2), dma(2), dma(npair), dma(npair), dma(npair), dma(npair), dma(npair), dma(npair),
        dma(npair), dma(npair), dma(2), dma(2 * nhead), dma(2 * nhead), dma(nhead), dma(nhead),
        dma(nseq), dma(nseq),
    ]
    whole = pl.BlockSpec(memory_space=pltpu.VMEM)
    return tuple(pl.pallas_call(
        functools.partial(kernel, nseq, nhead, norm),
        out_shape=(
            jax.ShapeDtypeStruct((tok, channels), BF16),
            jax.ShapeDtypeStruct((heads, tok), F32),
            jax.ShapeDtypeStruct((2, tok, state), F32),
            jax.ShapeDtypeStruct((2, heads), F32),
        ),
        in_specs=[whole] * 8 + [pl.BlockSpec(memory_space=pltpu.SMEM), whole],
        out_specs=(whole,) * 4,
        scratch_shapes=scratch,
        compiler_params=pltpu.CompilerParams(
            collective_id=0, has_side_effects=True, vmem_limit_bytes=48 << 20
        ),
    )(
        x_quant, scale_exp, dt_raw, dt_bias.reshape(1, heads), a_log.reshape(1, heads),
        skip_weight.reshape(1, heads), b_proj, c_proj, doc_starts, grad_out,
    ))


def solution(mesh):
    in_specs = (
        P("seq", "head"),
        P("head", "seq"),
        P("head", "seq"),
        P("head"),
        P("head"),
        P("head"),
        P("seq", None),
        P("seq", None),
        P("seq", None),
        P("seq", "head"),
    )
    out_specs = (P("seq", "head"), P("head", "seq"), P(None, "seq", None), P(None, "head"))
    return jax.shard_map(local, mesh=mesh, in_specs=in_specs, out_specs=out_specs, check_vma=False)
```

time: 352 us -> 67.3 us (0.19)
  waiting for transfers between devices: 242 us -> 0 us
  Pallas kernels: 0 us -> 57.9 us
  blocking collectives: 52.5 us -> 0 us
  other arithmetic: 17.7 us -> 0 us
  matrix products: 16.3 us -> 0 us
  between operations: 15.4 us -> 0.68 us
    all_gather x2 -> x0, waiting for transfers between devices: 213 us -> none  [carried_in(): gathered = jax.tree.map(lambda a: lax.all_gather(a, axis), part)]
    pallas_call x0 -> x1, Pallas kernels: none -> 57.9 us  [local(): pl.pallas_call(functools.partial(kernel, nseq, nhead, norm), out_shape=(j...]
    psum x1 -> x0, blocking collectives: 28.8 us -> none  [local(): totals = lax.psum(jnp.stack([alog_part, skip_part]), 'seq')]
    psum x1 -> x0, waiting for transfers between devices: 28.3 us -> none  [local(): grad_bc = lax.psum(jnp.stack([grad_b, grad_c]), 'head')]
    unnamed x1 -> x0, blocking collectives: 23.6 us -> none
    dot_general x11 -> x0, matrix products: 16.3 us -> none  [the longest x1 3.07 us: within_block(): jnp.einsum('htp,hsp->hts', grads_group, inputs_group, precision=highest)]
    add x8 -> x0, other arithmetic: 10.2 us -> none  [the longest x7 10.1 us: chain_step(): latter[1] + latter[0][:, None, None] * earlier[1]]
    unnamed x26 -> x24, local copies, waits for them, and re-layouts: 4.77 us -> 8.28 us
  transfers between devices with their start and end apart: 3 -> 0, of which waited for: 3 -> 0; matrix products, arithmetic and copies ran while one was open for 4% -> 0% of each run, Pallas kernels for 0% -> 0%
where the time goes in v1:
time: 67.3 us; the launch traced here: 66.9 us
  Pallas kernels  57.9 us (86%)
  local copies, waits for them, and re-layouts  8.28 us (12%)
  between operations  0.68 us (1%)
    pallas_call x1, Pallas kernels, local(): pl.pallas_call(functools.partial(kernel, nseq, nhead, norm), out_shape=(j...  57.9 us
    unnamed x24, local copies, waits for them, and re-layouts  8.28 us

profile of v1, /device:TPU:0, one launch (start us, length us, event | category | flops | bytes accessed | tf_op | source)
XLA Modules:
  0.0 66.9 jit_solution(4800406687658419377)
XLA Ops:
  0.6 0.0 copy-start.9
  0.6 0.0 copy-start.6
  0.7 0.0 copy-start.7
  0.7 0.0 copy-start.8
  0.7 0.6 copy-done.9
  1.3 0.0 copy-done.6
  1.3 0.0 copy-done.7
  1.3 0.0 copy-done.8
  1.3 0.0 copy-start
  1.3 1.0 %copy-done = bf16[128,2048]{1,0:T(8,128)(2,1)S(1)} copy-done((bf16[128,2048]{1,0:T(8,128)(2,1)S(1)}, bf16[128,2048]{1,0:T(8,128)(2,1)}, u32[]{:S(2)}) %copy-start) | copy-done | bytes 524312
  2.4 0.0 copy-start.1
  2.4 1.0 %copy-done.1 = bf16[128,2048]{1,0:T(8,128)(2,1)S(1)} copy-done((bf16[128,2048]{1,0:T(8,128)(2,1)S(1)}, bf16[128,2048]{1,0:T(8,128)(2,1)}, u32[]{:S(2)}) %copy-start.1) | copy-done | bytes 524312
  3.4 0.0 copy-start.2
  3.4 0.8 %copy-done.2 = bf16[128,128]{1,0:T(8,128)(2,1)S(1)} copy-done((bf16[128,128]{1,0:T(8,128)(2,1)S(1)}, bf16[128,128]{1,0:T(8,128)(2,1)}, u32[]{:S(2)}) %copy-start.2) | copy-done | bytes 32792
  4.2 0.0 copy-start.3
  4.2 0.8 %copy-done.3 = bf16[128,128]{1,0:T(8,128)(2,1)S(1)} copy-done((bf16[128,128]{1,0:T(8,128)(2,1)S(1)}, bf16[128,128]{1,0:T(8,128)(2,1)}, u32[]{:S(2)}) %copy-start.3) | copy-done | bytes 32792
  4.9 0.0 copy-start.4
  4.9 0.7 %copy-done.4 = s32[16,128]{1,0:T(8,128)S(1)} copy-done((s32[16,128]{1,0:T(8,128)S(1)}, s32[16,128]{1,0:T(8,128)}, u32[]{:S(2)}) %copy-start.4) | copy-done | bytes 8216
  5.6 0.0 copy-start.5
  5.6 0.7 %copy-done.5 = bf16[32,128]{1,0:T(8,128)(2,1)S(1)} copy-done((bf16[32,128]{1,0:T(8,128)(2,1)S(1)}, bf16[32,128]{1,0:T(8,128)(2,1)}, u32[]{:S(2)}) %copy-start.5) | copy-done | bytes 8216
  6.3 57.9 %shard_map.129 = (bf16[128,2048]{1,0:T(8,128)(2,1)S(1)}, f32[32,128]{1,0:T(8,128)S(1)}, f32[2,128,128]{2,1,0:T(8,128)S(1)}, f32[2,32]{1,0:T(2,128)S(1)}) custom-call(bf16[128,2048]{1,0:T(8,128)(2,1)S(1)} %copy-done, s32[16,128]{1,0:T(8,128)S(1)} %copy-done.4, bf16[32,128]{1,0:T(8,128)(2,1)S(1)} %copy-done.5, f32[1,32]{1,0:T(1,128)S(1)} %bitcast.3, ...), custom_call_target="tpu_custom_call" | custom-call | tf_op jit(solution)/shard_map/pallas_call | solution.py:470
  64.2 0.8 %copy.18 = bf16[128,2048]{1,0:T(8,128)(2,1)} copy(bf16[128,2048]{1,0:T(8,128)(2,1)S(1)} %get-tuple-element.8) | data formatting | bytes 1048576
  65.0 0.6 copy.19
  65.6 0.7 copy.20
  66.3 0.6 copy.21
Async XLA Ops:
  0.6 0.7 copy-start.9
  0.6 0.7 copy-start.6
  0.7 0.7 copy-start.7
  0.7 0.7 %copy-start.8 = (f32[32]{0:T(128)S(1)}, f32[32]{0:T(128)}, u32[]{:S(2)}) copy-start(f32[32]{0:T(128)} %param.15) | copy-start | bytes 388
  1.3 1.0 %copy-start = (bf16[128,2048]{1,0:T(8,128)(2,1)S(1)}, bf16[128,2048]{1,0:T(8,128)(2,1)}, u32[]{:S(2)}) copy-start(bf16[128,2048]{1,0:T(8,128)(2,1)} %x_ref.1) | copy-start | bytes 1572868
  2.4 1.0 %copy-start.1 = (bf16[128,2048]{1,0:T(8,128)(2,1)S(1)}, bf16[128,2048]{1,0:T(8,128)(2,1)}, u32[]{:S(2)}) copy-start(bf16[128,2048]{1,0:T(8,128)(2,1)} %g_ref.1) | copy-start | bytes 1572868
  3.4 0.8 %copy-start.2 = (bf16[128,128]{1,0:T(8,128)(2,1)S(1)}, bf16[128,128]{1,0:T(8,128)(2,1)}, u32[]{:S(2)}) copy-start(bf16[128,128]{1,0:T(8,128)(2,1)} %b_ref.1) | copy-start | bytes 98308
  4.2 0.8 %copy-start.3 = (bf16[128,128]{1,0:T(8,128)(2,1)S(1)}, bf16[128,128]{1,0:T(8,128)(2,1)}, u32[]{:S(2)}) copy-start(bf16[128,128]{1,0:T(8,128)(2,1)} %c_ref.1) | copy-start | bytes 98308
  4.9 0.7 %copy-start.4 = (s32[16,128]{1,0:T(8,128)S(1)}, s32[16,128]{1,0:T(8,128)}, u32[]{:S(2)}) copy-start(s32[16,128]{1,0:T(8,128)} %sc_ref.1) | copy-start | bytes 24580
  5.6 0.7 %copy-start.5 = (bf16[32,128]{1,0:T(8,128)(2,1)S(1)}, bf16[32,128]{1,0:T(8,128)(2,1)}, u32[]{:S(2)}) copy-start(bf16[32,128]{1,0:T(8,128)(2,1)} %dt_ref.1) | copy-start | bytes 24580

commit v2 on v1

--- a/solution.py
+++ b/solution.py
@@ -38,18 +38,14 @@
     return mm(a, high, dims) + mm(a, low, dims)
 
 
-def mm3(a, b, dims):
-    a_high, a_low = split(a)
-    b_high, b_low = split(b)
-    return mm(a_high, b_high, dims) + (mm(a_high, b_low, dims) + mm(a_low, b_high, dims))
-
-
 def kernel(
     nseq, nhead, norm,
-    x_ref, sc_ref, dt_ref, bias_ref, alog_ref, skip_ref, b_ref, c_ref, doc_ref, g_ref,
+    x_hbm, sc_hbm, dt_hbm, b_hbm, c_hbm, g_hbm, bias_ref, alog_ref, skip_ref, doc_ref,
     gx_out, dt_out, bc_out, hg_out,
-    fac, steps, cums, rates, sigm, skips, meta, msend, bcf, xgs, xg, kern, same, first, last,
-    xs_s, ge_s, exit_s, loc, es, rs_, er, rr, gxa, gxr, kg, cx, skp, ct, sg, sgr, bcp, red, gat, hgp,
+    x_ref, sc_ref, dt_ref, b_ref, c_ref, g_ref,
+    fac, steps, cums, rates, sigm, skips, meta, msend, bcf, xgs, xg, kern, same, first, last, cols,
+    twice, turned, step_s, enter_s, exit_s, ds_s, w_s, xs_s, ge_s, loc, es, rs_, er, rr, gxa, gxr,
+    kg, cx, ends, skp, ct, sg, sgr, ctc, sgc, bcp, red, gat, hgp, in_sems,
     meta_sems, bc_sems, xg_send, xg_recv, e_send, e_recv, r_send, r_recv, gx_send, gx_recv,
     sg_sems, red_send, red_recv, gat_send, gat_recv, hg_send, hg_recv,
 ):
@@ -63,6 +59,14 @@
     half = heads // 2
     npair = half // 2
 
+    fetches = [
+        pltpu.make_async_copy(src, dst, in_sems.at[i])
+        for i, (src, dst) in enumerate((
+            (sc_hbm, sc_ref), (b_hbm, b_ref), (c_hbm, c_ref), (dt_hbm, dt_ref), (x_hbm, x_ref), (g_hbm, g_ref),
+        ))
+    ]
+    for fetch in fetches:
+        fetch.start()
     barrier = pltpu.get_barrier_semaphore()
     for j in range(1, nseq):
         pl.semaphore_signal(barrier, inc=1, device_id=(lax.rem(me + j, nseq), hd), device_id_type=MESH)
@@ -97,6 +101,8 @@
     def gx_copy(k):
         return remote(gxa.at[oth, k], gxr.at[k], gx_send.at[k], gx_recv.at[k], across)
 
+    for fetch in fetches[:4]:
+        fetch.wait()
     bcf[par, 0] = b_ref[...].astype(F32)
     bcf[par, 1] = c_ref[...].astype(F32)
     fac[...] = jnp.left_shift(jnp.int32(1), sc_ref[...] + 8).astype(F32) / 256.0
@@ -126,6 +132,8 @@
         count = count + (row_id >= doc_ref[0, j]).astype(F32)
     mine = pl.ds(pl.multiple_of(par * half, half), half)
     theirs = pl.ds(pl.multiple_of(oth * half, half), half)
+    for fetch in fetches[4:]:
+        fetch.wait()
     meta[par, 0:half] = steps[mine]
     meta[par, half:2 * half] = cums[mine]
     meta[par, 2 * half:2 * half + 8] = count
@@ -160,6 +168,8 @@
     lax.fori_loop(0, npair, own_pair, 0)
     kg[...] = jnp.zeros_like(kg)
     cx[...] = jnp.zeros_like(cx)
+    ctc[...] = jnp.zeros_like(ctc)
+    sgc[...] = jnp.zeros_like(sgc)
 
     @pl.when(z == 0)
     def _():
@@ -169,54 +179,69 @@
     def _():
         rr[...] = jnp.zeros_like(rr)
 
+    lane_a = t_lane < HEAD_DIM
+
+    def row_of(q, row):
+        return meta[q, pl.ds(row, 1), :]
+
+    def prepare(q):
+        seg_row = jnp.broadcast_to(meta[q, 2 * half:2 * half + 1, :], (tok, tok))
+        padded = jnp.concatenate([meta[q], jnp.zeros((tok - 2 * half - 8, tok), F32)], axis=0).T
+        cols[...] = padded
+        seg_col = jnp.broadcast_to(padded[:, 2 * half:2 * half + 1], (tok, tok))
+        end = meta[q, 2 * half:2 * half + 1, tok - 1:tok]
+        same[...] = ((t_sub <= t_lane) & (seg_row == seg_col)).astype(F32)
+        first[...] = (seg_col == 0.0).astype(F32)
+        last[...] = (seg_col == end).astype(F32)
+        for i in range(2):
+            whole = bcf[q, i].astype(BF16)
+            flat = bcf[q, i].T.astype(BF16)
+            twice[q, i] = jnp.concatenate([whole, whole], axis=1)
+            turned[q, i] = jnp.concatenate([flat, flat], axis=1)
+        kern[q] = mm(bcf[q, 0].astype(BF16), bcf[q, 1].astype(BF16), ROWS)
+
+        def pair(k, carry):
+            rolled = pltpu.roll(cols[...], lax.rem(tok - 2 * k, tok), 1)
+            step_cols = [jnp.broadcast_to(rolled[:, i:i + 1], (tok, tok)) for i in range(2)]
+            cum_cols = [jnp.broadcast_to(rolled[:, half + i:half + i + 1], (tok, tok)) for i in range(2)]
+            cum = jnp.where(lane_a, cum_cols[0], cum_cols[1])
+            step_s[k, q] = jnp.where(lane_a, step_cols[0], step_cols[1])
+            enter_s[k, q] = jnp.exp(cum) * first[...]
+            exit_s[k, q] = jnp.exp(cum[tok - 1:tok, :] - cum) * last[...]
+            mask = same[...] > 0.5
+            for i in range(2):
+                gap = row_of(q, half + 2 * k + i) - cum_cols[i]
+                decay = jnp.exp(jnp.where(mask, gap, -1e30))
+                ds_s[k, q, i] = decay * step_cols[i]
+                high, low = split(decay * kern[q])
+                w_s[k, q, :, i * tok:(i + 1) * tok] = high
+                w_s[k, q, :, (2 + i) * tok:(3 + i) * tok] = low
+            return carry
+
+        lax.fori_loop(0, npair, pair, 0)
+
+    prepare(par)
     bc_copy(oth).wait_recv()
     meta_copy(oth).wait_recv()
-
-    def pair_of(q, row):
-        return meta[q, pl.ds(row, 1), :]
-
-    for q in range(2):
-        seg_row = jnp.broadcast_to(meta[q, 2 * half:2 * half + 1, :], (tok, tok))
-        seg_col = seg_row.T
-        end = meta[q, 2 * half:2 * half + 1, tok - 1:tok]
-        same[q] = ((t_sub >= t_lane) & (seg_row == seg_col)).astype(F32)
-        first[q] = (seg_col == 0.0).astype(F32)
-        last[q] = (seg_col == end).astype(F32)
-        kern[q] = mm(bcf[q, 1].astype(BF16), bcf[q, 0].astype(BF16), ROWS)
-
-    def lanes_of(a, b):
-        return jnp.concatenate(
-            [jnp.broadcast_to(a, (HEAD_DIM, tok)), jnp.broadcast_to(b, (HEAD_DIM, tok))], axis=0
-        ).T
-
-    def slab_decay(q, k):
-        whole = 1.0 - jnp.minimum(meta[q, 2 * half:2 * half + 1, tok - 1:tok], 1.0)
-        ends = [
-            jnp.broadcast_to(
-                jnp.exp(pair_of(q, half + 2 * k + s)[:, tok - 1:tok]) * whole, (HEAD_DIM, tok)
-            )
-            for s in range(2)
-        ]
-        return jnp.concatenate(ends, axis=0)
+    prepare(oth)
+
+    def decay_of(q, k):
+        return enter_s[k, q, tok - 1:tok, :]
 
     def local_part(k):
         xg_copy(oth, k).wait_recv()
         states, grads = [], []
         for q in range(2):
-            cum = lanes_of(pair_of(q, half + 2 * k), pair_of(q, half + 2 * k + 1))
-            step = lanes_of(pair_of(q, 2 * k), pair_of(q, 2 * k + 1))
-            enter_w = jnp.exp(cum) * first[q]
-            exit_w = jnp.exp(cum[tok - 1:tok, :] - cum) * last[q]
-            xs = exit_w * (step * xg[q, k, 0])
-            ge = enter_w * xg[q, k, 1]
-            xs_s[k, q] = xs
-            ge_s[k, q] = ge
-            exit_s[k, q] = exit_w
-            states.append(mm2(xs, bcf[q, 0].astype(BF16), COLS))
-            grads.append(mm2(ge, bcf[q, 1].astype(BF16), COLS))
-        d0, d1 = slab_decay(0, k), slab_decay(1, k)
-        loc[k, 0] = d1 * states[0] + states[1]
-        loc[k, 1] = d0 * grads[1] + grads[0]
+            xs = exit_s[k, q] * (step_s[k, q] * xg[q, k, 0])
+            ge = enter_s[k, q] * xg[q, k, 1]
+            xs_two = jnp.concatenate(split(xs), axis=0)
+            ge_two = jnp.concatenate(split(ge), axis=0)
+            xs_s[k, q] = xs_two
+            ge_s[k, q] = ge_two
+            states.append(mm(turned[q, 0], xs_two, PLAIN))
+            grads.append(mm(turned[q, 1], ge_two, PLAIN))
+        loc[k, 0] = decay_of(1, k) * states[0] + states[1]
+        loc[k, 1] = decay_of(0, k) * grads[1] + grads[0]
         loc[k, 2] = states[0]
         loc[k, 3] = grads[1]
 
@@ -227,7 +252,7 @@
 
         @pl.when(z < zs - 1)
         def _():
-            es[k] = slab_decay(0, k) * slab_decay(1, k) * er[k] + loc[k, 0]
+            es[k] = (decay_of(0, k) * decay_of(1, k)) * er[k] + loc[k, 0]
             e_copy(k).start()
 
     def backward_part(k):
@@ -237,64 +262,63 @@
 
         @pl.when(z > 0)
         def _():
-            rs_[k] = slab_decay(0, k) * slab_decay(1, k) * rr[k] + loc[k, 1]
+            rs_[k] = (decay_of(0, k) * decay_of(1, k)) * rr[k] + loc[k, 1]
             r_copy(k).start()
 
-    lane_a = t_lane < HEAD_DIM
+    def wide(a):
+        return jnp.concatenate([a[0:tok], a[tok:2 * tok]], axis=1)
+
+    def corner(high, low):
+        return jnp.concatenate(
+            [jnp.concatenate([high, high], axis=1), jnp.concatenate([low, low], axis=1)], axis=0
+        )
 
     def final_part(k):
         entry0, exit1 = er[k], rr[k]
-        decays = [slab_decay(0, k), slab_decay(1, k)]
-        entries = [entry0, decays[0] * entry0 + loc[k, 2]]
-        exits = [decays[1] * exit1 + loc[k, 3], exit1]
-        skip_rows = [skips[pl.ds(par * half + 2 * k + s, 1), :] for s in range(2)]
+        entries = [entry0, decay_of(0, k) * entry0 + loc[k, 2]]
+        exits = [decay_of(1, k) * exit1 + loc[k, 3], exit1]
+        skip_rows = [skips[pl.ds(par * half + 2 * k + i, 1), :] for i in range(2)]
         skip_lanes = jnp.where(lane_a[0:1], skip_rows[0], skip_rows[1])
         skip_sum = jnp.zeros((1, tok), F32)
         for q in range(2):
             x_val, g_val = xg[q, k, 0], xg[q, k, 1]
-            bq, cq = bcf[q, 0].astype(BF16), bcf[q, 1].astype(BF16)
-            xs, ge, exit_w = xs_s[k, q], ge_s[k, q], exit_s[k, q]
+            exit_w, step = exit_s[k, q], step_s[k, q]
             entry, leave = entries[q], exits[q]
-            read = mm2r(cq, entry, ROWS)
-            back = mm2r(bq, leave, ROWS)
-            cx[q, 1] += mm3(ge, entry, PLAIN)
-            cx[q, 0] += mm3(xs, leave, PLAIN)
-            exit_terms = xs * back
+            e_high, e_low = split(entry)
+            l_high, l_low = split(leave)
+            read = mm(twice[q, 1], jnp.concatenate([e_high, e_low], axis=0), PLAIN)
+            back = mm(twice[q, 0], jnp.concatenate([l_high, l_low], axis=0), PLAIN)
+            cx[q, 1] += mm(wide(ge_s[k, q]), corner(e_high, e_low), ROWS)
+            cx[q, 0] += mm(wide(xs_s[k, q]), corner(l_high, l_low), ROWS)
             g_two = jnp.concatenate(
                 [jnp.where(lane_a, g_val, 0.0), jnp.where(lane_a, 0.0, g_val)], axis=0
             ).astype(BF16)
-            scores = mm(g_two, x_val.astype(BF16), ROWS)
-            weights, flows = [], []
-            kern_q, mask = kern[q], same[q] > 0.5
-            total = jnp.zeros((tok, tok), F32)
-            for s in range(2):
-                step_row = pair_of(q, 2 * k + s)
-                row = jnp.broadcast_to(pair_of(q, half + 2 * k + s), (tok, tok))
-                decay = jnp.exp(jnp.where(mask, row.T - row, -1e30))
-                part = decay * (scores[s * tok:(s + 1) * tok] * step_row)
-                total = total + part
-                weights.append(decay * kern_q)
-                flows.append(part * kern_q)
-            kg[q] += total
-            inner = mm2(jnp.concatenate(weights, axis=0), g_two, COLS)
-            input_total = inner + exit_w * back
-            sums = (ge * read - exit_terms).T
-            moved = (input_total * x_val).T
-            exit_sum = jnp.sum(exit_terms, axis=0, keepdims=True)
-            both = leave * entry * decays[q]
-            at_end = t_lane[0:1] == tok - 1
-            for s in range(2):
-                span = slice(s * HEAD_DIM, (s + 1) * HEAD_DIM)
-                ending = jnp.sum(exit_sum[:, span], keepdims=True) + jnp.sum(both[span], keepdims=True)
-                cumul = (
-                    jnp.sum(flows[s].T - flows[s], axis=0, keepdims=True)
-                    + jnp.sum(sums[span], axis=0, keepdims=True)
-                    + jnp.where(at_end, ending, 0.0)
-                )
-                ct[q, pl.ds(2 * k + s, 1), :] = cumul
-                sg[q, pl.ds(2 * k + s, 1), :] = jnp.sum(moved[span], axis=0, keepdims=True)
+            scores = mm(x_val.astype(BF16), g_two, ROWS)
+            inner = mm(w_s[k, q], jnp.concatenate([g_two, g_two], axis=0), PLAIN)
+            kern_q = kern[q]
+            parts = [scores[:, i * tok:(i + 1) * tok] * ds_s[k, q, i] for i in range(2)]
+            kg[q] += parts[0] + parts[1]
+            flows = [part * kern_q for part in parts]
+            back_w = exit_w * back
+            input_total = inner + back_w
+            exit_terms = (step * x_val) * back_w
+            through = (enter_s[k, q] * g_val) * read - exit_terms
+            moved = input_total * x_val
+            ends[q, pl.ds(k, 1), :] = jnp.sum(
+                exit_terms + leave * entry * decay_of(q, k), axis=0, keepdims=True
+            )
+            ct_cols, sg_cols = ctc[q], sgc[q]
+            for i in range(2):
+                mine_only = lane_a if i == 0 else ~lane_a
+                ct_col = jnp.sum(jnp.where(mine_only, through, 0.0) - flows[i], axis=1, keepdims=True)
+                sg_col = jnp.sum(jnp.where(mine_only, moved, 0.0), axis=1, keepdims=True)
+                spot = t_lane == 2 * k + i
+                ct_cols = jnp.where(spot, ct_col, ct_cols)
+                sg_cols = jnp.where(spot, sg_col, sg_cols)
+                ct[q, pl.ds(2 * k + i, 1), :] = jnp.sum(flows[i], axis=0, keepdims=True)
+            ctc[q] = ct_cols
+            sgc[q] = sg_cols
             skip_sum = skip_sum + jnp.sum(g_val * x_val, axis=0, keepdims=True)
-            step = lanes_of(pair_of(q, 2 * k), pair_of(q, 2 * k + 1))
             gxa[q, k] = input_total * step + skip_lanes * g_val
         skp[pl.ds(k, 1), :] = skip_sum
         gx_copy(k).start()
@@ -327,8 +351,10 @@
     lax.fori_loop(0, npair + zs - 1, lap, 0)
 
     for q in range(2):
-        bcp[q, 0:tok] = mm2(kg[q], bcf[q, 1].astype(BF16), COLS) + cx[q, 0]
-        bcp[q, tok:2 * tok] = mm2(kg[q], bcf[q, 0].astype(BF16), PLAIN) + cx[q, 1]
+        b_sum, c_sum = cx[q, 0], cx[q, 1]
+        b_sum, c_sum = b_sum[:, 0:tok] + b_sum[:, tok:], c_sum[:, 0:tok] + c_sum[:, tok:]
+        bcp[q, 0:tok] = mm2(kg[q], bcf[q, 1].astype(BF16), PLAIN) + b_sum
+        bcp[q, tok:2 * tok] = mm2(kg[q], bcf[q, 0].astype(BF16), COLS) + c_sum
     piece = 2 * tok // nhead
     here = par * nhead + hd
     base = me - par
@@ -346,16 +372,25 @@
     lower = (t_sub >= t_lane).astype(F32)
     rate_own = rates[mine]
     alog_sum = jnp.zeros((half, 1), F32)
+    h_sub = lax.broadcasted_iota(jnp.int32, (half, tok), 0)
+    h_lane = lax.broadcasted_iota(jnp.int32, (half, tok), 1)
+    pick = lax.div(h_lane, HEAD_DIM) == lax.rem(h_sub, 2)
     for q in range(2):
+        per_pair = ends[q]
+        ending = jnp.sum(
+            jnp.where(pick, jnp.broadcast_to(per_pair[:, None, :], (npair, 2, tok)).reshape(half, tok), 0.0),
+            axis=1, keepdims=True,
+        )
+        total = ct[q] + ctc[q].T[0:half] + jnp.where(h_lane == tok - 1, ending, 0.0)
+        sg[q] = sgc[q].T[0:half]
         decay_grad = lax.dot_general(
-            ct[q], lower, (PLAIN, ((), ())), precision=HIGHEST, preferred_element_type=F32
+            total, lower, (PLAIN, ((), ())), precision=HIGHEST, preferred_element_type=F32
         )
         sg[q] = sg[q] - rate_own * decay_grad
         alog_sum = alog_sum - jnp.sum(decay_grad * meta[q, 0:half] * rate_own, axis=1, keepdims=True)
     sg_copy = remote(sg.at[oth], sgr, sg_sems.at[0], sg_sems.at[1], across)
     sg_copy.start()
-    h_sub = lax.broadcasted_iota(jnp.int32, (half, tok), 0)
-    h_lane = lax.broadcasted_iota(jnp.int32, (half, tok), 1) - par * half
+    h_lane = h_lane - par * half
     alog_row = jnp.sum(jnp.where(h_sub == h_lane, alog_sum, 0.0), axis=0, keepdims=True)
     skip_all = skp[...]
     skip_a = jnp.sum(skip_all[:, 0:HEAD_DIM], axis=1, keepdims=True)
@@ -444,24 +479,32 @@
     vmem = lambda *shape: pltpu.VMEM(shape, F32)
     dma = lambda n: pltpu.SemaphoreType.DMA((n,))
     sq = (tok, state)
+    half16 = lambda *shape: pltpu.VMEM(shape, BF16)
     scratch = [
+        half16(tok, channels), pltpu.VMEM(scale_exp.shape, jnp.int32), half16(heads, tok),
+        half16(*sq), half16(*sq), half16(tok, channels),
         vmem(scale_exp.shape[0], tok),
         vmem(heads, tok), vmem(heads, tok), vmem(heads, tok), vmem(heads, tok), vmem(heads, tok),
         vmem(2, 2 * half + 8, tok), vmem(2 * half + 8, tok),
         vmem(2, 2, *sq),
         vmem(npair, 2, *sq), vmem(2, npair, 2, *sq),
-        vmem(2, *sq), vmem(2, *sq), vmem(2, *sq), vmem(2, *sq),
+        vmem(2, *sq), vmem(*sq), vmem(*sq), vmem(*sq), vmem(*sq),
+        half16(2, 2, tok, 2 * state), half16(2, 2, state, 2 * tok),
         vmem(npair, 2, *sq), vmem(npair, 2, *sq), vmem(npair, 2, *sq),
+        vmem(npair, 2, 2, *sq), half16(npair, 2, tok, 4 * tok),
+        half16(npair, 2, 2 * tok, state), half16(npair, 2, 2 * tok, state),
         vmem(npair, 4, *sq),
         vmem(npair, *sq), vmem(npair, *sq), vmem(npair, *sq), vmem(npair, *sq),
         vmem(2, npair, *sq), vmem(npair, *sq),
-        vmem(2, *sq), vmem(2, 2, *sq),
-        vmem(npair, tok),
+        vmem(2, *sq), vmem(2, 2, tok, 2 * state),
+        vmem(2, npair, tok), vmem(npair, tok),
         vmem(2, half, tok), vmem(2, half, tok), vmem(half, tok),
+        vmem(2, *sq), vmem(2, *sq),
         vmem(2, 2 * tok, state),
         vmem(2 * nhead, 2 * tok // nhead, state),
         vmem(nhead, 2 * tok // nhead, state),
         vmem(nseq, 8, tok),
+        dma(6),
         dma(2), dma(2), dma(npair), dma(npair), dma(npair), dma(npair), dma(npair), dma(npair),
         dma(npair), dma(npair), dma(2), dma(2 * nhead), dma(2 * nhead), dma(nhead), dma(nhead),
         dma(nseq), dma(nseq),
@@ -475,15 +518,15 @@
             jax.ShapeDtypeStruct((2, tok, state), F32),
             jax.ShapeDtypeStruct((2, heads), F32),
         ),
-        in_specs=[whole] * 8 + [pl.BlockSpec(memory_space=pltpu.SMEM), whole],
+        in_specs=[pl.BlockSpec(memory_space=pl.ANY)] * 6 + [whole] * 3 + [pl.BlockSpec(memory_space=pltpu.SMEM)],
         out_specs=(whole,) * 4,
         scratch_shapes=scratch,
         compiler_params=pltpu.CompilerParams(
             collective_id=0, has_side_effects=True, vmem_limit_bytes=48 << 20
         ),
     )(
-        x_quant, scale_exp, dt_raw, dt_bias.reshape(1, heads), a_log.reshape(1, heads),
-        skip_weight.reshape(1, heads), b_proj, c_proj, doc_starts, grad_out,
+        x_quant, scale_exp, dt_raw, b_proj, c_proj, grad_out, dt_bias.reshape(1, heads),
+        a_log.reshape(1, heads), skip_weight.reshape(1, heads), doc_starts,
     ))
 
 

time: 67.3 us -> 66.3 us (0.985)
  Pallas kernels: 57.9 us -> 56.9 us
    pallas_call x1, Pallas kernels: 57.9 us -> 56.9 us  [local(): pl.pallas_call(functools.partial(kernel, nseq, nhead, norm), out_shape=(j...]
where the time goes in v2:
time: 66.3 us; the launch traced here: 65.9 us
  Pallas kernels  56.9 us (86%)
  local copies, waits for them, and re-layouts  8.28 us (12%)
  between operations  0.68 us (1%)
    pallas_call x1, Pallas kernels, local(): pl.pallas_call(functools.partial(kernel, nseq, nhead, norm), out_shape=(j...  56.9 us
    unnamed x24, local copies, waits for them, and re-layouts  8.28 us

profile of v2, /device:TPU:0, one launch (start us, length us, event | category | flops | bytes accessed | tf_op | source)
XLA Modules:
  0.0 65.9 jit_solution(6075192555031753656)
XLA Ops:
  0.6 0.0 copy-start.9
  0.6 0.0 copy-start.6
  0.7 0.0 copy-start.7
  0.7 0.0 copy-start.8
  0.7 0.6 copy-done.9
  1.3 0.0 copy-done.6
  1.3 0.0 copy-done.7
  1.3 0.0 copy-done.8
  1.3 0.0 copy-start
  1.3 1.0 %copy-done = bf16[128,2048]{1,0:T(8,128)(2,1)S(1)} copy-done((bf16[128,2048]{1,0:T(8,128)(2,1)S(1)}, bf16[128,2048]{1,0:T(8,128)(2,1)}, u32[]{:S(2)}) %copy-start) | copy-done | bytes 524312
  2.4 0.0 copy-start.1
  2.4 1.0 %copy-done.1 = bf16[128,2048]{1,0:T(8,128)(2,1)S(1)} copy-done((bf16[128,2048]{1,0:T(8,128)(2,1)S(1)}, bf16[128,2048]{1,0:T(8,128)(2,1)}, u32[]{:S(2)}) %copy-start.1) | copy-done | bytes 524312
  3.4 0.0 copy-start.2
  3.4 0.8 %copy-done.2 = bf16[128,128]{1,0:T(8,128)(2,1)S(1)} copy-done((bf16[128,128]{1,0:T(8,128)(2,1)S(1)}, bf16[128,128]{1,0:T(8,128)(2,1)}, u32[]{:S(2)}) %copy-start.2) | copy-done | bytes 32792
  4.2 0.0 copy-start.3
  4.2 0.8 %copy-done.3 = bf16[128,128]{1,0:T(8,128)(2,1)S(1)} copy-done((bf16[128,128]{1,0:T(8,128)(2,1)S(1)}, bf16[128,128]{1,0:T(8,128)(2,1)}, u32[]{:S(2)}) %copy-start.3) | copy-done | bytes 32792
  4.9 0.0 copy-start.4
  4.9 0.7 %copy-done.4 = s32[16,128]{1,0:T(8,128)S(1)} copy-done((s32[16,128]{1,0:T(8,128)S(1)}, s32[16,128]{1,0:T(8,128)}, u32[]{:S(2)}) %copy-start.4) | copy-done | bytes 8216
  5.6 0.0 copy-start.5
  5.6 0.7 %copy-done.5 = bf16[32,128]{1,0:T(8,128)(2,1)S(1)} copy-done((bf16[32,128]{1,0:T(8,128)(2,1)S(1)}, bf16[32,128]{1,0:T(8,128)(2,1)}, u32[]{:S(2)}) %copy-start.5) | copy-done | bytes 8216
  6.3 56.9 %shard_map.129 = (bf16[128,2048]{1,0:T(8,128)(2,1)S(1)}, f32[32,128]{1,0:T(8,128)S(1)}, f32[2,128,128]{2,1,0:T(8,128)S(1)}, f32[2,32]{1,0:T(2,128)S(1)}) custom-call(bf16[128,2048]{1,0:T(8,128)(2,1)S(1)} %copy-done, s32[16,128]{1,0:T(8,128)S(1)} %copy-done.4, bf16[32,128]{1,0:T(8,128)(2,1)S(1)} %copy-done.5, bf16[128,128]{1,0:T(8,128)(2,1)S(1)} %copy-done.2, ...), custom_call_target="tpu_custom_call" | custom-call | tf_op jit(solution)/shard_map/pallas_call | solution.py:513
  63.3 0.8 %copy.18 = bf16[128,2048]{1,0:T(8,128)(2,1)} copy(bf16[128,2048]{1,0:T(8,128)(2,1)S(1)} %get-tuple-element.8) | data formatting | bytes 1048576
  64.1 0.6 copy.19
  64.7 0.7 copy.20
  65.3 0.6 copy.21
Async XLA Ops:
  0.6 0.7 copy-start.9
  0.6 0.7 %copy-start.6 = (f32[32]{0:T(128)S(1)}, f32[32]{0:T(128)}, u32[]{:S(2)}) copy-start(f32[32]{0:T(128)} %param.13) | copy-start | bytes 388
  0.7 0.7 %copy-start.7 = (f32[32]{0:T(128)S(1)}, f32[32]{0:T(128)}, u32[]{:S(2)}) copy-start(f32[32]{0:T(128)} %param.14) | copy-start | bytes 388
  0.7 0.7 %copy-start.8 = (f32[32]{0:T(128)S(1)}, f32[32]{0:T(128)}, u32[]{:S(2)}) copy-start(f32[32]{0:T(128)} %param.15) | copy-start | bytes 388
  1.3 1.0 %copy-start = (bf16[128,2048]{1,0:T(8,128)(2,1)S(1)}, bf16[128,2048]{1,0:T(8,128)(2,1)}, u32[]{:S(2)}) copy-start(bf16[128,2048]{1,0:T(8,128)(2,1)} %x_hbm.1) | copy-start | bytes 1572868
  2.4 1.0 %copy-start.1 = (bf16[128,2048]{1,0:T(8,128)(2,1)S(1)}, bf16[128,2048]{1,0:T(8,128)(2,1)}, u32[]{:S(2)}) copy-start(bf16[128,2048]{1,0:T(8,128)(2,1)} %g_hbm.1) | copy-start | bytes 1572868
  3.4 0.8 %copy-start.2 = (bf16[128,128]{1,0:T(8,128)(2,1)S(1)}, bf16[128,128]{1,0:T(8,128)(2,1)}, u32[]{:S(2)}) copy-start(bf16[128,128]{1,0:T(8,128)(2,1)} %b_hbm.1) | copy-start | bytes 98308
  4.2 0.8 %copy-start.3 = (bf16[128,128]{1,0:T(8,128)(2,1)S(1)}, bf16[128,128]{1,0:T(8,128)(2,1)}, u32[]{:S(2)}) copy-start(bf16[128,128]{1,0:T(8,128)(2,1)} %c_hbm.1) | copy-start | bytes 98308
  4.9 0.7 %copy-start.4 = (s32[16,128]{1,0:T(8,128)S(1)}, s32[16,128]{1,0:T(8,128)}, u32[]{:S(2)}) copy-start(s32[16,128]{1,0:T(8,128)} %sc_hbm.1) | copy-start | bytes 24580
  5.6 0.7 %copy-start.5 = (bf16[32,128]{1,0:T(8,128)(2,1)S(1)}, bf16[32,128]{1,0:T(8,128)(2,1)}, u32[]{:S(2)}) copy-start(bf16[32,128]{1,0:T(8,128)(2,1)} %dt_hbm.1) | copy-start | bytes 24580

commit v3 on v2

v3 whole, which is shorter than its diff:
```python
import functools
import math

import jax
import jax.numpy as jnp
from jax import lax
from jax.experimental import pallas as pl
from jax.experimental.pallas import tpu as pltpu
from jax.sharding import PartitionSpec as P

HEAD_DIM = 64
MESH = pl.DeviceIdType.MESH
F32 = jnp.float32
BF16 = jnp.bfloat16
HIGHEST = lax.Precision.HIGHEST

ROWS = ((1,), (1,))
COLS = ((0,), (0,))
PLAIN = ((1,), (0,))


def mm(a, b, dims):
    return lax.dot_general(a, b, (dims, ((), ())), preferred_element_type=F32)


def split(a):
    high = a.astype(BF16)
    return high, (a - high.astype(F32)).astype(BF16)


def mm2(a, b, dims):
    high, low = split(a)
    return mm(high, b, dims) + mm(low, b, dims)


def mm2r(a, b, dims):
    high, low = split(b)
    return mm(a, high, dims) + mm(a, low, dims)


def kernel(
    nseq, nhead, norm,
    x_hbm, sc_hbm, dt_hbm, b_hbm, c_hbm, g_hbm, bias_ref, alog_ref, skip_ref, doc_ref,
    gx_out, dt_out, bc_out, hg_out,
    x_ref, sc_ref, dt_ref, b_ref, c_ref, g_ref,
    fac, steps, rates, skips, meta, cf, gg, xv, kern, same, first, last, cols,
    twice, turned, step_s, enter_s, exit_s, ds_s, w_s, xs_s, ge_s, loc, es, rs_, er, rr,
    kg, bx, cx, ends, skp, ct, ctc, sgc, far, near, own_out, oth_out, red_own, red_oth, gat, hgp,
    in_sems, c_sems, meta_sems, g_send, g_recv, e_send, e_recv, r_send, r_recv, far_sems,
    own_send, own_recv, oth_send, oth_recv, gat_send, gat_recv, hg_send, hg_recv,
):
    me, hd = lax.axis_index("seq"), lax.axis_index("head")
    par, z = lax.rem(me, 2), lax.div(me, 2)
    zs = nseq // 2
    oth = 1 - par
    partner = me + 1 - 2 * par
    tok = x_ref.shape[0]
    heads = dt_ref.shape[0]
    npair = heads // 2
    step_at = heads + 8

    fetches = [
        pltpu.make_async_copy(src, dst, in_sems.at[i])
        for i, (src, dst) in enumerate((
            (c_hbm, c_ref), (dt_hbm, dt_ref), (g_hbm, g_ref), (sc_hbm, sc_ref), (b_hbm, b_ref), (x_hbm, x_ref),
        ))
    ]
    for fetch in fetches:
        fetch.start()
    barrier = pltpu.get_barrier_semaphore()
    for j in range(1, nseq):
        pl.semaphore_signal(barrier, inc=1, device_id=(lax.rem(me + j, nseq), hd), device_id_type=MESH)
    for j in range(1, nhead):
        there = lax.rem(hd + j, nhead)
        pl.semaphore_signal(barrier, inc=1, device_id=(me, there), device_id_type=MESH)
        pl.semaphore_signal(barrier, inc=1, device_id=(partner, there), device_id_type=MESH)

    def remote(src, dst, send, recv, device):
        return pltpu.make_async_remote_copy(
            src_ref=src, dst_ref=dst, send_sem=send, recv_sem=recv,
            device_id=device, device_id_type=MESH,
        )

    across = (partner, hd)

    def c_copy(slab):
        return remote(cf.at[slab], cf.at[slab], c_sems.at[0], c_sems.at[1], across)

    def meta_copy(slab):
        return remote(meta.at[slab], meta.at[slab], meta_sems.at[0], meta_sems.at[1], across)

    def g_copy(slab, k):
        return remote(gg.at[slab, k], gg.at[slab, k], g_send.at[k], g_recv.at[k], across)

    def e_copy(k):
        return remote(es.at[k], er.at[k], e_send.at[k], e_recv.at[k], (lax.rem(me + 2, nseq), hd))

    def r_copy(k):
        return remote(rs_.at[k], rr.at[k], r_send.at[k], r_recv.at[k], (lax.rem(me + nseq - 2, nseq), hd))

    sub = lax.broadcasted_iota(jnp.int32, (heads, heads), 0)
    lane = lax.broadcasted_iota(jnp.int32, (heads, heads), 1)

    def column(ref):
        return jnp.sum(jnp.where(sub == lane, ref[...], 0.0), axis=1, keepdims=True)

    t_sub = lax.broadcasted_iota(jnp.int32, (tok, tok), 0)
    t_lane = lax.broadcasted_iota(jnp.int32, (tok, tok), 1)
    lane_a = t_lane < HEAD_DIM
    rate = jnp.exp(column(alog_ref))
    rates[...] = jnp.broadcast_to(rate, (heads, tok))
    skips[...] = jnp.broadcast_to(column(skip_ref), (heads, tok))
    row_id = lax.broadcasted_iota(jnp.int32, (8, tok), 1)
    count = jnp.zeros((8, tok), F32)
    for j in range(doc_ref.shape[1]):
        count = count + (row_id >= doc_ref[0, j]).astype(F32)
    bias = column(bias_ref)
    fetches[0].wait()
    cf[par] = c_ref[...].astype(F32)
    fetches[1].wait()
    pre = dt_ref[...].astype(F32) + bias
    step_all = jnp.maximum(pre, 0.0) + jnp.log1p(jnp.exp(-jnp.abs(pre)))
    steps[...] = step_all
    upper = (t_sub <= t_lane).astype(F32)
    meta[par, 0:heads] = lax.dot_general(
        -rate * step_all, upper, (PLAIN, ((), ())), precision=HIGHEST, preferred_element_type=F32
    )
    meta[par, heads:heads + 8] = count
    fetches[2].wait()

    pl.semaphore_wait(barrier, nseq - 1 + 2 * (nhead - 1))
    meta_copy(par).start()
    c_copy(par).start()

    def lanes_at(k):
        return pl.ds(pl.multiple_of(k * tok, tok), tok)

    def send_pair(k, carry):
        gg[par, k] = g_ref[:, lanes_at(k)].astype(F32)
        g_copy(par, k).start()
        return carry

    lax.fori_loop(0, npair, send_pair, 0)
    for fetch in fetches[3:]:
        fetch.wait()
    fac[...] = jnp.left_shift(jnp.int32(1), sc_ref[...] + 8).astype(F32) / 256.0
    kg[...] = jnp.zeros_like(kg)
    bx[...] = jnp.zeros_like(bx)
    cx[...] = jnp.zeros_like(cx)
    ctc[...] = jnp.zeros_like(ctc)
    sgc[...] = jnp.zeros_like(sgc)

    @pl.when(z == 0)
    def _():
        er[...] = jnp.zeros_like(er)

    @pl.when(z == zs - 1)
    def _():
        rr[...] = jnp.zeros_like(rr)

    def row_of(q, row):
        return meta[q, pl.ds(row, 1), :]

    def prepare(q, rest):
        rows = jnp.concatenate([meta[q], rest], axis=0)
        flat = rows.T
        cols[q] = flat
        seg_col = jnp.broadcast_to(flat[:, heads:heads + 1], (tok, tok))
        first[q] = (seg_col == 0.0).astype(F32)
        whole = cf[q].astype(BF16)
        c_flat = cf[q].T.astype(BF16)
        twice[q] = jnp.concatenate([whole, whole], axis=1)
        turned[q] = jnp.concatenate([c_flat, c_flat], axis=1)
        return seg_col

    def enter_of(q, k):
        rolled = pltpu.roll(cols[q], lax.rem(tok - 2 * k, tok), 1)
        cum_cols = [jnp.broadcast_to(rolled[:, i:i + 1], (tok, tok)) for i in range(2)]
        cum = jnp.where(lane_a, cum_cols[0], cum_cols[1])
        enter_s[q, k] = jnp.exp(cum) * first[q]
        return rolled, cum_cols, cum

    seg_own = prepare(par, jnp.concatenate([steps[...], jnp.zeros((tok - 2 * heads - 8, tok), F32)], axis=0))
    seg_row = jnp.broadcast_to(meta[par, heads:heads + 1, :], (tok, tok))
    same[...] = ((t_sub <= t_lane) & (seg_row == seg_own)).astype(F32)
    last[...] = (seg_own == meta[par, heads:heads + 1, tok - 1:tok]).astype(F32)
    b_own = b_ref[...]
    b_flat = b_own.astype(F32).T.astype(BF16)
    twice[2] = jnp.concatenate([b_own, b_own], axis=1)
    turned[2] = jnp.concatenate([b_flat, b_flat], axis=1)
    kern[...] = mm(b_own, c_ref[...], ROWS)

    def own_pair(k, carry):
        factor = jnp.broadcast_to(fac[pl.ds(k, 1), :], (tok, tok)).T
        x_val = x_ref[:, lanes_at(k)].astype(F32) * factor
        xv[k] = x_val
        rolled, cum_cols, cum = enter_of(par, k)
        step_cols = [jnp.broadcast_to(rolled[:, step_at + i:step_at + i + 1], (tok, tok)) for i in range(2)]
        step = jnp.where(lane_a, step_cols[0], step_cols[1])
        exit_w = jnp.exp(cum[tok - 1:tok, :] - cum) * last[...]
        step_s[k] = step
        exit_s[k] = exit_w
        mask = same[...] > 0.5
        for i in range(2):
            gap = row_of(par, 2 * k + i) - cum_cols[i]
            decay = jnp.exp(jnp.where(mask, gap, -1e30))
            ds_s[k, i] = decay * step_cols[i]
            high, low = split(decay * kern[...])
            w_s[k, :, i * tok:(i + 1) * tok] = high
            w_s[k, :, (2 + i) * tok:(3 + i) * tok] = low
        xs_two = jnp.concatenate(split(exit_w * (step * x_val)), axis=0)
        xs_s[k] = xs_two
        loc[k, 2] = mm(turned[2], xs_two, PLAIN)
        ge_s[par, k] = jnp.concatenate(split(enter_s[par, k] * gg[par, k]), axis=0)
        return carry

    lax.fori_loop(0, npair, own_pair, 0)
    meta_copy(oth).wait_recv()
    c_copy(oth).wait_recv()
    prepare(oth, jnp.zeros((tok - heads - 8, tok), F32))

    def decay_of(q, k):
        return enter_s[q, k, tok - 1:tok, :]

    def local_part(k):
        enter_of(oth, k)
        g_copy(oth, k).wait_recv()
        ge_s[oth, k] = jnp.concatenate(split(enter_s[oth, k] * gg[oth, k]), axis=0)
        grads = [mm(turned[q], ge_s[q, k], PLAIN) for q in range(2)]
        onward = jnp.where(par == 0, decay_of(1, k), 1.0)
        loc[k, 0] = onward * loc[k, 2]
        loc[k, 1] = decay_of(0, k) * grads[1] + grads[0]
        loc[k, 3] = grads[1]

    def forward_part(k):
        @pl.when(z > 0)
        def _():
            e_copy(k).wait_recv()

        @pl.when(z < zs - 1)
        def _():
            es[k] = (decay_of(0, k) * decay_of(1, k)) * er[k] + loc[k, 0]
            e_copy(k).start()

    def backward_part(k):
        @pl.when(z < zs - 1)
        def _():
            r_copy(k).wait_recv()

        @pl.when(z > 0)
        def _():
            rs_[k] = (decay_of(0, k) * decay_of(1, k)) * rr[k] + loc[k, 1]
            r_copy(k).start()

    def wide(a):
        return jnp.concatenate([a[0:tok], a[tok:2 * tok]], axis=1)

    def corner(high, low):
        return jnp.concatenate(
            [jnp.concatenate([high, high], axis=1), jnp.concatenate([low, low], axis=1)], axis=0
        )

    def final_part(k):
        entry0, exit1 = er[k], rr[k]
        entry1 = decay_of(0, k) * entry0 + jnp.where(par == 0, loc[k, 2], 0.0)
        exit0 = decay_of(1, k) * exit1 + loc[k, 3]
        early = par == 0
        entry_own, entry_oth = jnp.where(early, entry0, entry1), jnp.where(early, entry1, entry0)
        leave_own, leave_oth = jnp.where(early, exit0, exit1), jnp.where(early, exit1, exit0)

        def entering(q, entry):
            high, low = split(entry)
            read = mm(twice[q], jnp.concatenate([high, low], axis=0), PLAIN)
            cx[q] += mm(wide(ge_s[q, k]), corner(high, low), ROWS)
            return (enter_s[q, k] * gg[q, k]) * read

        def place(cols_ref, q, full, minus):
            kept = cols_ref[q]
            for i in range(2):
                part = jnp.where(lane_a if i == 0 else ~lane_a, full, 0.0)
                if minus is not None:
                    part = part - minus[i]
                kept = jnp.where(t_lane == 2 * k + i, jnp.sum(part, axis=1, keepdims=True), kept)
            cols_ref[q] = kept

        through = entering(oth, entry_oth)
        place(ctc, oth, through, None)
        ends[oth, pl.ds(k, 1), :] = jnp.sum(leave_oth * entry_oth, axis=0, keepdims=True) * decay_of(oth, k)

        x_val, g_val = xv[k], gg[par, k]
        exit_w, step = exit_s[k], step_s[k]
        l_high, l_low = split(leave_own)
        back = mm(twice[2], jnp.concatenate([l_high, l_low], axis=0), PLAIN)
        bx[...] += mm(wide(xs_s[k]), corner(l_high, l_low), ROWS)
        g_two = jnp.concatenate(
            [jnp.where(lane_a, g_val, 0.0), jnp.where(lane_a, 0.0, g_val)], axis=0
        ).astype(BF16)
        scores = mm(x_val.astype(BF16), g_two, ROWS)
        inner = mm(w_s[k], jnp.concatenate([g_two, g_two], axis=0), PLAIN)
        kern_own = kern[...]
        parts = [scores[:, i * tok:(i + 1) * tok] * ds_s[k, i] for i in range(2)]
        kg[...] += parts[0] + parts[1]
        flows = [part * kern_own for part in parts]
        back_w = exit_w * back
        input_total = inner + back_w
        exit_terms = (step * x_val) * back_w
        place(ctc, par, entering(par, entry_own) - exit_terms, flows)
        place(sgc, 0, input_total * x_val, None)
        ends[par, pl.ds(k, 1), :] = (
            jnp.sum(exit_terms, axis=0, keepdims=True)
            + jnp.sum(leave_own * entry_own, axis=0, keepdims=True) * decay_of(par, k)
        )
        for i in range(2):
            ct[pl.ds(2 * k + i, 1), :] = jnp.sum(flows[i], axis=0, keepdims=True)
        skp[pl.ds(k, 1), :] = jnp.sum(g_val * x_val, axis=0, keepdims=True)
        skip_rows = [skips[pl.ds(2 * k + i, 1), :] for i in range(2)]
        skip_lanes = jnp.where(lane_a[0:1], skip_rows[0], skip_rows[1])
        gx_out[:, lanes_at(k)] = (input_total * step + skip_lanes * g_val).astype(BF16)

    def lap(i, carry):
        @pl.when(i < npair)
        def _():
            local_part(i)

        ahead = i - z

        @pl.when((ahead >= 0) & (ahead < npair))
        def _():
            forward_part(ahead)

        behind = i - (zs - 1 - z)

        @pl.when((behind >= 0) & (behind < npair))
        def _():
            backward_part(behind)

        @pl.when(i >= zs - 1)
        def _():
            final_part(i - (zs - 1))

        return carry

    lax.fori_loop(0, npair + zs - 1, lap, 0)

    def folded(a):
        return a[:, 0:tok] + a[:, tok:]

    piece = tok // nhead
    state = b_ref.shape[1]
    oth_out[...] = folded(cx[oth]).reshape(nhead, piece, state)

    def oth_copy(to, slot):
        return remote(oth_out.at[to], red_oth.at[slot], oth_send.at[to], oth_recv.at[slot], (partner, to))

    def own_copy(to, slot):
        return remote(own_out.at[to], red_own.at[slot], own_send.at[to], own_recv.at[slot], (me, to))

    for j in range(nhead):
        oth_copy(lax.rem(hd + j, nhead), hd).start()

    h_sub = lax.broadcasted_iota(jnp.int32, (heads, tok), 0)
    h_lane = lax.broadcasted_iota(jnp.int32, (heads, tok), 1)
    pick = lax.div(h_lane, HEAD_DIM) == lax.rem(h_sub, 2)

    def cumul_of(q):
        per_head = jnp.broadcast_to(ends[q][:, None, :], (npair, 2, tok)).reshape(heads, tok)
        ending = jnp.sum(jnp.where(pick, per_head, 0.0), axis=1, keepdims=True)
        return ctc[q].T[0:heads] + jnp.where(h_lane == tok - 1, ending, 0.0)

    far[...] = cumul_of(oth)
    far_copy = remote(far, near, far_sems.at[0], far_sems.at[1], across)
    far_copy.start()

    own_out[:, 0] = (mm2(kg[...], c_ref[...], PLAIN) + folded(bx[...])).reshape(nhead, piece, state)
    own_out[:, 1] = (mm2(kg[...], b_ref[...], COLS) + folded(cx[par])).reshape(nhead, piece, state)
    for j in range(1, nhead):
        own_copy(lax.rem(hd + j, nhead), hd).start()

    mine = ct[...] + cumul_of(par)
    lower = (t_sub >= t_lane).astype(F32)
    far_copy.wait_recv()
    decay_grad = lax.dot_general(
        mine + near[...], lower, (PLAIN, ((), ())), precision=HIGHEST, preferred_element_type=F32
    )
    step_all = steps[...]
    alog_sum = -jnp.sum(decay_grad * step_all * rates[...], axis=1, keepdims=True)
    alog_row = jnp.sum(jnp.where(h_sub == h_lane, alog_sum, 0.0), axis=0, keepdims=True)
    skip_all = skp[...]
    skip_a = jnp.sum(skip_all[:, 0:HEAD_DIM], axis=1, keepdims=True)
    skip_b = jnp.sum(skip_all[:, HEAD_DIM:], axis=1, keepdims=True)
    k_sub, k_lane = 2 * h_sub[0:npair], h_lane[0:npair]
    skip_row = jnp.sum(
        jnp.where(k_sub == k_lane, skip_a, 0.0) + jnp.where(k_sub + 1 == k_lane, skip_b, 0.0),
        axis=0, keepdims=True,
    )
    r_sub = lax.broadcasted_iota(jnp.int32, (8, tok), 0)
    hgp[me] = jnp.where(r_sub == 0, alog_row, jnp.where(r_sub == 1, skip_row, 0.0))

    def hg_copy(to, slot):
        return remote(hgp.at[slot], hgp.at[slot], hg_send.at[to], hg_recv.at[slot], (to, hd))

    for j in range(1, nseq):
        hg_copy(lax.rem(me + j, nseq), me).start()

    red_own[hd] = own_out[hd]
    for j in range(nhead):
        other = lax.rem(hd + j, nhead)
        oth_copy(other, other).wait_recv()
    for j in range(1, nhead):
        other = lax.rem(hd + j, nhead)
        own_copy(other, other).wait_recv()
    b_c = jnp.sum(red_own[...], axis=0)
    gat[hd, 0] = b_c[0]
    gat[hd, 1] = b_c[1] + jnp.sum(red_oth[...], axis=0)

    def gat_copy(to, slot):
        return remote(gat.at[slot], gat.at[slot], gat_send.at[to], gat_recv.at[slot], (me, to))

    for j in range(1, nhead):
        gat_copy(lax.rem(hd + j, nhead), hd).start()

    sigmoid = 1.0 / (1.0 + jnp.exp(-(dt_ref[...].astype(F32) + bias)))
    dt_out[...] = (sgc[0].T[0:heads] - rates[...] * decay_grad) * sigmoid
    for j in range(1, nseq):
        other = lax.rem(me + j, nseq)
        hg_copy(other, other).wait_recv()
    hg_out[...] = jnp.sum(hgp[...], axis=0)[0:2, 0:heads] * norm
    for j in range(1, nhead):
        other = lax.rem(hd + j, nhead)
        gat_copy(other, other).wait_recv()
    for i in range(2):
        bc_out[i] = gat[:, i].reshape(tok, state)

    meta_copy(par).wait_send()
    c_copy(par).wait_send()
    far_copy.wait_send()

    def drain(k, carry):
        g_copy(par, k).wait_send()

        @pl.when(z < zs - 1)
        def _():
            e_copy(k).wait_send()

        @pl.when(z > 0)
        def _():
            r_copy(k).wait_send()

        return carry

    lax.fori_loop(0, npair, drain, 0)
    for j in range(nhead):
        oth_copy(lax.rem(hd + j, nhead), hd).wait_send()
    for j in range(1, nhead):
        own_copy(lax.rem(hd + j, nhead), hd).wait_send()
        gat_copy(lax.rem(hd + j, nhead), hd).wait_send()
    for j in range(1, nseq):
        hg_copy(lax.rem(me + j, nseq), me).wait_send()


def local(
    x_quant, scale_exp, dt_raw, dt_bias, a_log, skip_weight, b_proj, c_proj, doc_starts, grad_out
):
    nseq, nhead = lax.axis_size("seq"), lax.axis_size("head")
    tok, channels = x_quant.shape
    heads = dt_raw.shape[0]
    state = b_proj.shape[1]
    npair, piece = heads // 2, tok // nhead
    norm = 1.0 / math.sqrt(tok * nseq * HEAD_DIM)
    vmem = lambda *shape: pltpu.VMEM(shape, F32)
    half16 = lambda *shape: pltpu.VMEM(shape, BF16)
    dma = lambda n: pltpu.SemaphoreType.DMA((n,))
    sq = (tok, state)
    scratch = [
        half16(tok, channels), pltpu.VMEM(scale_exp.shape, jnp.int32), half16(heads, tok),
        half16(*sq), half16(*sq), half16(tok, channels),
        vmem(scale_exp.shape[0], tok),
        vmem(heads, tok), vmem(heads, tok), vmem(heads, tok),
        vmem(2, heads + 8, tok), vmem(2, *sq),
        vmem(2, npair, *sq), vmem(npair, *sq),
        vmem(*sq), vmem(*sq), vmem(2, *sq), vmem(*sq), vmem(2, *sq),
        half16(3, tok, 2 * state), half16(3, state, 2 * tok),
        vmem(npair, *sq), vmem(2, npair, *sq), vmem(npair, *sq),
        vmem(npair, 2, *sq), half16(npair, tok, 4 * tok),
        half16(npair, 2 * tok, state), half16(2, npair, 2 * tok, state),
        vmem(npair, 4, *sq),
        vmem(npair, *sq), vmem(npair, *sq), vmem(npair, *sq), vmem(npair, *sq),
        vmem(*sq), vmem(tok, 2 * state), vmem(2, tok, 2 * state),
        vmem(2, npair, tok), vmem(npair, tok), vmem(heads, tok),
        vmem(2, *sq), vmem(1, *sq), vmem(heads, tok), vmem(heads, tok),
        vmem(nhead, 2, piece, state), vmem(nhead, piece, state),
        vmem(nhead, 2, piece, state), vmem(nhead, piece, state),
        vmem(nhead, 2, piece, state), vmem(nseq, 8, tok),
        dma(6), dma(2), dma(2), dma(npair), dma(npair), dma(npair), dma(npair), dma(npair), dma(npair),
        dma(2), dma(nhead), dma(nhead), dma(nhead), dma(nhead), dma(nhead), dma(nhead),
        dma(nseq), dma(nseq),
    ]
    whole = pl.BlockSpec(memory_space=pltpu.VMEM)
    return tuple(pl.pallas_call(
        functools.partial(kernel, nseq, nhead, norm),
        out_shape=(
            jax.ShapeDtypeStruct((tok, channels), BF16),
            jax.ShapeDtypeStruct((heads, tok), F32),
            jax.ShapeDtypeStruct((2, tok, state), F32),
            jax.ShapeDtypeStruct((2, heads), F32),
        ),
        in_specs=[pl.BlockSpec(memory_space=pl.ANY)] * 6 + [whole] * 3 + [pl.BlockSpec(memory_space=pltpu.SMEM)],
        out_specs=(whole,) * 4,
        scratch_shapes=scratch,
        compiler_params=pltpu.CompilerParams(
            collective_id=0, has_side_effects=True, vmem_limit_bytes=60 << 20
        ),
    )(
        x_quant, scale_exp, dt_raw, b_proj, c_proj, grad_out, dt_bias.reshape(1, heads),
        a_log.reshape(1, heads), skip_weight.reshape(1, heads), doc_starts,
    ))


def solution(mesh):
    in_specs = (
        P("seq", "head"),
        P("head", "seq"),
        P("head", "seq"),
        P("head"),
        P("head"),
        P("head"),
        P("seq", None),
        P("seq", None),
        P("seq", None),
        P("seq", "head"),
    )
    out_specs = (P("seq", "head"), P("head", "seq"), P(None, "seq", None), P(None, "head"))
    return jax.shard_map(local, mesh=mesh, in_specs=in_specs, out_specs=out_specs, check_vma=False)
```

time: 66.3 us -> 86.5 us (1.30)
  Pallas kernels: 56.9 us -> 81.9 us
  local copies, waits for them, and re-layouts: 8.28 us -> 3.76 us
    pallas_call x1, Pallas kernels: 56.9 us -> 81.9 us  [local(): pl.pallas_call(functools.partial(kernel, nseq, nhead, norm), out_shape=(j...]
    unnamed x24 -> x10, local copies, waits for them, and re-layouts: 8.28 us -> 3.76 us
where the time goes in v3:
time: 86.5 us; the launch traced here: 86.3 us
  Pallas kernels  81.9 us (95%)
  local copies, waits for them, and re-layouts  3.76 us (4%)
    pallas_call x1, Pallas kernels, local(): pl.pallas_call(functools.partial(kernel, nseq, nhead, norm), out_shape=(j...  81.9 us
    unnamed x10, local copies, waits for them, and re-layouts  3.76 us

profile of v3, /device:TPU:0, one launch (start us, length us, event | category | flops | bytes accessed | tf_op | source)
XLA Modules:
  0.0 86.3 jit_solution(7409034001094236121)
XLA Ops:
  0.6 81.9 %shard_map.129 = (bf16[128,2048]{1,0:T(8,128)(2,1)}, f32[32,128]{1,0:T(8,128)}, f32[2,128,128]{2,1,0:T(8,128)}, f32[2,32]{1,0:T(2,128)}) custom-call(bf16[128,2048]{1,0:T(8,128)(2,1)} %x_hbm.1, s32[16,128]{1,0:T(8,128)} %sc_hbm.1, bf16[32,128]{1,0:T(8,128)(2,1)} %dt_hbm.1, bf16[128,128]{1,0:T(8,128)(2,1)} %b_hbm.1, bf16[128,128]{1,0:T(8,128)(2,1)} %c_hbm.1, ...), custom_call_target="tpu_custom_call" | custom-call | tf_op jit(solution)/shard_map/pallas_call | solution.py:499
  82.5 0.0 copy-start.1
  82.5 0.0 copy-start
  82.5 1.9 %copy.18 = bf16[128,2048]{1,0:T(8,128)(2,1)} copy(bf16[128,2048]{1,0:T(8,128)(2,1)} %get-tuple-element.8) | data formatting | bytes 1048576
  84.4 0.0 copy-done.1
  84.4 0.6 copy.19
  85.1 0.0 copy-done
  85.1 0.0 copy-start.2
  85.1 0.7 copy.20
  85.7 0.0 copy-done.2
  85.7 0.6 copy.21
Async XLA Ops:
  82.5 1.9 %copy-start.1 = (f32[32,128]{1,0:T(8,128)S(1)}, f32[32,128]{1,0:T(8,128)}, u32[]{:S(2)}) copy-start(f32[32,128]{1,0:T(8,128)} %get-tuple-element.9) | copy-start | bytes 49156
  82.5 2.5 %copy-start = (f32[2,128,128]{2,1,0:T(8,128)S(1)}, f32[2,128,128]{2,1,0:T(8,128)}, u32[]{:S(2)}) copy-start(f32[2,128,128]{2,1,0:T(8,128)} %get-tuple-element.10) | copy-start | bytes 393220
  85.1 0.7 copy-start.2

commit v4 on v3

--- a/solution.py
+++ b/solution.py
@@ -9,6 +9,7 @@
 from jax.sharding import PartitionSpec as P
 
 HEAD_DIM = 64
+LAG = 2
 MESH = pl.DeviceIdType.MESH
 F32 = jnp.float32
 BF16 = jnp.bfloat16
@@ -44,7 +45,7 @@
     gx_out, dt_out, bc_out, hg_out,
     x_ref, sc_ref, dt_ref, b_ref, c_ref, g_ref,
     fac, steps, rates, skips, meta, cf, gg, xv, kern, same, first, last, cols,
-    twice, turned, step_s, enter_s, exit_s, ds_s, w_s, xs_s, ge_s, loc, es, rs_, er, rr,
+    twice, turned, step_s, enter_s, exit_s, inner_s, xs_s, ge_s, loc, es, rs_, er, rr,
     kg, bx, cx, ends, skp, ct, ctc, sgc, far, near, own_out, oth_out, red_own, red_oth, gat, hgp,
     in_sems, c_sems, meta_sems, g_send, g_recv, e_send, e_recv, r_send, r_recv, far_sems,
     own_send, own_recv, oth_send, oth_recv, gat_send, gat_recv, hg_send, hg_recv,
@@ -190,7 +191,14 @@
     turned[2] = jnp.concatenate([b_flat, b_flat], axis=1)
     kern[...] = mm(b_own, c_ref[...], ROWS)
 
-    def own_pair(k, carry):
+    meta_copy(oth).wait_recv()
+    c_copy(oth).wait_recv()
+    prepare(oth, jnp.zeros((tok - heads - 8, tok), F32))
+
+    def decay_of(q, k):
+        return enter_s[q, k, tok - 1:tok, :]
+
+    def own_part(k):
         factor = jnp.broadcast_to(fac[pl.ds(k, 1), :], (tok, tok)).T
         x_val = x_ref[:, lanes_at(k)].astype(F32) * factor
         xv[k] = x_val
@@ -200,35 +208,46 @@
         exit_w = jnp.exp(cum[tok - 1:tok, :] - cum) * last[...]
         step_s[k] = step
         exit_s[k] = exit_w
+        xs_two = jnp.concatenate(split(exit_w * (step * x_val)), axis=0)
+        xs_s[k] = xs_two
+        own_state = mm(turned[2], xs_two, PLAIN)
+        loc[k, 2] = own_state
+        g_val = gg[par, k]
+        ge_s[par, k] = jnp.concatenate(split(enter_s[par, k] * g_val), axis=0)
+        g_two = jnp.concatenate(
+            [jnp.where(lane_a, g_val, 0.0), jnp.where(lane_a, 0.0, g_val)], axis=0
+        ).astype(BF16)
+        scores = mm(x_val.astype(BF16), g_two, ROWS)
         mask = same[...] > 0.5
+        kern_own = kern[...]
+        total, highs, lows, flows = None, [], [], []
         for i in range(2):
             gap = row_of(par, 2 * k + i) - cum_cols[i]
             decay = jnp.exp(jnp.where(mask, gap, -1e30))
-            ds_s[k, i] = decay * step_cols[i]
-            high, low = split(decay * kern[...])
-            w_s[k, :, i * tok:(i + 1) * tok] = high
-            w_s[k, :, (2 + i) * tok:(3 + i) * tok] = low
-        xs_two = jnp.concatenate(split(exit_w * (step * x_val)), axis=0)
-        xs_s[k] = xs_two
-        loc[k, 2] = mm(turned[2], xs_two, PLAIN)
-        ge_s[par, k] = jnp.concatenate(split(enter_s[par, k] * gg[par, k]), axis=0)
-        return carry
-
-    lax.fori_loop(0, npair, own_pair, 0)
-    meta_copy(oth).wait_recv()
-    c_copy(oth).wait_recv()
-    prepare(oth, jnp.zeros((tok - heads - 8, tok), F32))
-
-    def decay_of(q, k):
-        return enter_s[q, k, tok - 1:tok, :]
+            part = scores[:, i * tok:(i + 1) * tok] * (decay * step_cols[i])
+            high, low = split(decay * kern_own)
+            highs.append(high)
+            lows.append(low)
+            flow = part * kern_own
+            flows.append(flow)
+            total = part if total is None else total + part
+            ct[pl.ds(2 * k + i, 1), :] = jnp.sum(flow, axis=0, keepdims=True)
+        kg[...] += total
+        kept = ctc[par]
+        for i in range(2):
+            kept = jnp.where(t_lane == 2 * k + i, -jnp.sum(flows[i], axis=1, keepdims=True), kept)
+        ctc[par] = kept
+        inner_s[k] = mm(
+            jnp.concatenate(highs + lows, axis=1), jnp.concatenate([g_two, g_two], axis=0), PLAIN
+        )
+        skp[pl.ds(k, 1), :] = jnp.sum(g_val * x_val, axis=0, keepdims=True)
 
     def local_part(k):
         enter_of(oth, k)
+        loc[k, 0] = jnp.where(par == 0, decay_of(1, k), 1.0) * loc[k, 2]
         g_copy(oth, k).wait_recv()
         ge_s[oth, k] = jnp.concatenate(split(enter_s[oth, k] * gg[oth, k]), axis=0)
         grads = [mm(turned[q], ge_s[q, k], PLAIN) for q in range(2)]
-        onward = jnp.where(par == 0, decay_of(1, k), 1.0)
-        loc[k, 0] = onward * loc[k, 2]
         loc[k, 1] = decay_of(0, k) * grads[1] + grads[0]
         loc[k, 3] = grads[1]
 
@@ -274,17 +293,16 @@
             cx[q] += mm(wide(ge_s[q, k]), corner(high, low), ROWS)
             return (enter_s[q, k] * gg[q, k]) * read
 
-        def place(cols_ref, q, full, minus):
+        def place(cols_ref, q, full):
             kept = cols_ref[q]
             for i in range(2):
                 part = jnp.where(lane_a if i == 0 else ~lane_a, full, 0.0)
-                if minus is not None:
-                    part = part - minus[i]
-                kept = jnp.where(t_lane == 2 * k + i, jnp.sum(part, axis=1, keepdims=True), kept)
+                part_sum = jnp.sum(part, axis=1, keepdims=True)
+                kept = kept + jnp.where(t_lane == 2 * k + i, part_sum, 0.0)
             cols_ref[q] = kept
 
         through = entering(oth, entry_oth)
-        place(ctc, oth, through, None)
+        place(ctc, oth, through)
         ends[oth, pl.ds(k, 1), :] = jnp.sum(leave_oth * entry_oth, axis=0, keepdims=True) * decay_of(oth, k)
 
         x_val, g_val = xv[k], gg[par, k]
@@ -292,27 +310,15 @@
         l_high, l_low = split(leave_own)
         back = mm(twice[2], jnp.concatenate([l_high, l_low], axis=0), PLAIN)
         bx[...] += mm(wide(xs_s[k]), corner(l_high, l_low), ROWS)
-        g_two = jnp.concatenate(
-            [jnp.where(lane_a, g_val, 0.0), jnp.where(lane_a, 0.0, g_val)], axis=0
-        ).astype(BF16)
-        scores = mm(x_val.astype(BF16), g_two, ROWS)
-        inner = mm(w_s[k], jnp.concatenate([g_two, g_two], axis=0), PLAIN)
-        kern_own = kern[...]
-        parts = [scores[:, i * tok:(i + 1) * tok] * ds_s[k, i] for i in range(2)]
-        kg[...] += parts[0] + parts[1]
-        flows = [part * kern_own for part in parts]
         back_w = exit_w * back
-        input_total = inner + back_w
+        input_total = inner_s[k] + back_w
         exit_terms = (step * x_val) * back_w
-        place(ctc, par, entering(par, entry_own) - exit_terms, flows)
-        place(sgc, 0, input_total * x_val, None)
+        place(ctc, par, entering(par, entry_own) - exit_terms)
+        place(sgc, 0, input_total * x_val)
         ends[par, pl.ds(k, 1), :] = (
             jnp.sum(exit_terms, axis=0, keepdims=True)
             + jnp.sum(leave_own * entry_own, axis=0, keepdims=True) * decay_of(par, k)
         )
-        for i in range(2):
-            ct[pl.ds(2 * k + i, 1), :] = jnp.sum(flows[i], axis=0, keepdims=True)
-        skp[pl.ds(k, 1), :] = jnp.sum(g_val * x_val, axis=0, keepdims=True)
         skip_rows = [skips[pl.ds(2 * k + i, 1), :] for i in range(2)]
         skip_lanes = jnp.where(lane_a[0:1], skip_rows[0], skip_rows[1])
         gx_out[:, lanes_at(k)] = (input_total * step + skip_lanes * g_val).astype(BF16)
@@ -320,27 +326,28 @@
     def lap(i, carry):
         @pl.when(i < npair)
         def _():
+            own_part(i)
             local_part(i)
 
-        ahead = i - z
+        ahead = i - LAG * z
 
         @pl.when((ahead >= 0) & (ahead < npair))
         def _():
             forward_part(ahead)
 
-        behind = i - (zs - 1 - z)
+        behind = i - LAG * (zs - 1 - z)
 
         @pl.when((behind >= 0) & (behind < npair))
         def _():
             backward_part(behind)
 
-        @pl.when(i >= zs - 1)
-        def _():
-            final_part(i - (zs - 1))
+        @pl.when(i >= LAG * (zs - 1))
+        def _():
+            final_part(i - LAG * (zs - 1))
 
         return carry
 
-    lax.fori_loop(0, npair + zs - 1, lap, 0)
+    lax.fori_loop(0, npair + LAG * (zs - 1), lap, 0)
 
     def folded(a):
         return a[:, 0:tok] + a[:, tok:]
@@ -481,7 +488,7 @@
         vmem(*sq), vmem(*sq), vmem(2, *sq), vmem(*sq), vmem(2, *sq),
         half16(3, tok, 2 * state), half16(3, state, 2 * tok),
         vmem(npair, *sq), vmem(2, npair, *sq), vmem(npair, *sq),
-        vmem(npair, 2, *sq), half16(npair, tok, 4 * tok),
+        vmem(npair, *sq),
         half16(npair, 2 * tok, state), half16(2, npair, 2 * tok, state),
         vmem(npair, 4, *sq),
         vmem(npair, *sq), vmem(npair, *sq), vmem(npair, *sq), vmem(npair, *sq),

time: 86.5 us -> 63.6 us (0.74)
  Pallas kernels: 81.9 us -> 59 us
    pallas_call x1, Pallas kernels: 81.9 us -> 59 us  [local(): pl.pallas_call(functools.partial(kernel, nseq, nhead, norm), out_shape=(j...]
where the time goes in v4:
time: 63.6 us; the launch traced here: 63.4 us
  Pallas kernels  59 us (93%)
  local copies, waits for them, and re-layouts  3.76 us (6%)
  between operations  0.66 us (1%)
    pallas_call x1, Pallas kernels, local(): pl.pallas_call(functools.partial(kernel, nseq, nhead, norm), out_shape=(j...  59 us
    unnamed x10, local copies, waits for them, and re-layouts  3.76 us

profile of v4, /device:TPU:0, one launch (start us, length us, event | category | flops | bytes accessed | tf_op | source)
XLA Modules:
  0.0 63.4 jit_solution(3424041406343714197)
XLA Ops:
  0.6 59.0 %shard_map.129 = (bf16[128,2048]{1,0:T(8,128)(2,1)}, f32[32,128]{1,0:T(8,128)}, f32[2,128,128]{2,1,0:T(8,128)}, f32[2,32]{1,0:T(2,128)}) custom-call(bf16[128,2048]{1,0:T(8,128)(2,1)} %x_hbm.1, s32[16,128]{1,0:T(8,128)} %sc_hbm.1, bf16[32,128]{1,0:T(8,128)(2,1)} %dt_hbm.1, bf16[128,128]{1,0:T(8,128)(2,1)} %b_hbm.1, bf16[128,128]{1,0:T(8,128)(2,1)} %c_hbm.1, ...), custom_call_target="tpu_custom_call" | custom-call | tf_op jit(solution)/shard_map/pallas_call | solution.py:506
  59.6 0.0 copy-start.1
  59.6 0.0 copy-start
  59.6 1.9 %copy.18 = bf16[128,2048]{1,0:T(8,128)(2,1)} copy(bf16[128,2048]{1,0:T(8,128)(2,1)} %get-tuple-element.8) | data formatting | bytes 1048576
  61.5 0.0 copy-done.1
  61.5 0.6 copy.19
  62.1 0.0 copy-done
  62.1 0.0 copy-start.2
  62.1 0.7 %copy.20 = f32[2,128,128]{2,1,0:T(8,128)} copy(f32[2,128,128]{2,1,0:T(8,128)S(1)} %copy-done) | data formatting | bytes 262144
  62.8 0.0 copy-done.2
  62.8 0.6 copy.21
Async XLA Ops:
  59.6 1.9 %copy-start.1 = (f32[32,128]{1,0:T(8,128)S(1)}, f32[32,128]{1,0:T(8,128)}, u32[]{:S(2)}) copy-start(f32[32,128]{1,0:T(8,128)} %get-tuple-element.9) | copy-start | bytes 49156
  59.6 2.5 %copy-start = (f32[2,128,128]{2,1,0:T(8,128)S(1)}, f32[2,128,128]{2,1,0:T(8,128)}, u32[]{:S(2)}) copy-start(f32[2,128,128]{2,1,0:T(8,128)} %get-tuple-element.10) | copy-start | bytes 393220
  62.1 0.7 %copy-start.2 = (f32[2,32]{1,0:T(2,128)S(1)}, f32[2,32]{1,0:T(2,128)}, u32[]{:S(2)}) copy-start(f32[2,32]{1,0:T(2,128)} %get-tuple-element.11) | copy-start | bytes 772

commit v5 on v4

--- a/solution.py
+++ b/solution.py
@@ -9,7 +9,7 @@
 from jax.sharding import PartitionSpec as P
 
 HEAD_DIM = 64
-LAG = 2
+LAG = 3
 MESH = pl.DeviceIdType.MESH
 F32 = jnp.float32
 BF16 = jnp.bfloat16
@@ -46,7 +46,7 @@
     x_ref, sc_ref, dt_ref, b_ref, c_ref, g_ref,
     fac, steps, rates, skips, meta, cf, gg, xv, kern, same, first, last, cols,
     twice, turned, step_s, enter_s, exit_s, inner_s, xs_s, ge_s, loc, es, rs_, er, rr,
-    kg, bx, cx, ends, skp, ct, ctc, sgc, far, near, own_out, oth_out, red_own, red_oth, gat, hgp,
+    kg, bx, cx, ends, skp, ct, ctf, ctc, sgc, far, near, own_out, oth_out, red_own, red_oth, gat, hgp,
     in_sems, c_sems, meta_sems, g_send, g_recv, e_send, e_recv, r_send, r_recv, far_sems,
     own_send, own_recv, oth_send, oth_recv, gat_send, gat_recv, hg_send, hg_recv,
 ):
@@ -149,6 +149,7 @@
     bx[...] = jnp.zeros_like(bx)
     cx[...] = jnp.zeros_like(cx)
     ctc[...] = jnp.zeros_like(ctc)
+    ctf[...] = jnp.zeros_like(ctf)
     sgc[...] = jnp.zeros_like(sgc)
 
     @pl.when(z == 0)
@@ -190,10 +191,6 @@
     twice[2] = jnp.concatenate([b_own, b_own], axis=1)
     turned[2] = jnp.concatenate([b_flat, b_flat], axis=1)
     kern[...] = mm(b_own, c_ref[...], ROWS)
-
-    meta_copy(oth).wait_recv()
-    c_copy(oth).wait_recv()
-    prepare(oth, jnp.zeros((tok - heads - 8, tok), F32))
 
     def decay_of(q, k):
         return enter_s[q, k, tok - 1:tok, :]
@@ -233,10 +230,10 @@
             total = part if total is None else total + part
             ct[pl.ds(2 * k + i, 1), :] = jnp.sum(flow, axis=0, keepdims=True)
         kg[...] += total
-        kept = ctc[par]
+        kept = ctf[...]
         for i in range(2):
-            kept = jnp.where(t_lane == 2 * k + i, -jnp.sum(flows[i], axis=1, keepdims=True), kept)
-        ctc[par] = kept
+            kept = jnp.where(t_lane == 2 * k + i, jnp.sum(flows[i], axis=1, keepdims=True), kept)
+        ctf[...] = kept
         inner_s[k] = mm(
             jnp.concatenate(highs + lows, axis=1), jnp.concatenate([g_two, g_two], axis=0), PLAIN
         )
@@ -245,7 +242,6 @@
     def local_part(k):
         enter_of(oth, k)
         loc[k, 0] = jnp.where(par == 0, decay_of(1, k), 1.0) * loc[k, 2]
-        g_copy(oth, k).wait_recv()
         ge_s[oth, k] = jnp.concatenate(split(enter_s[oth, k] * gg[oth, k]), axis=0)
         grads = [mm(turned[q], ge_s[q, k], PLAIN) for q in range(2)]
         loc[k, 1] = decay_of(0, k) * grads[1] + grads[0]
@@ -323,31 +319,51 @@
         skip_lanes = jnp.where(lane_a[0:1], skip_rows[0], skip_rows[1])
         gx_out[:, lanes_at(k)] = (input_total * step + skip_lanes * g_val).astype(BF16)
 
+    own_part(0)
+    meta_copy(oth).wait_recv()
+    c_copy(oth).wait_recv()
+    prepare(oth, jnp.zeros((tok - heads - 8, tok), F32))
+    delay = 1 + LAG * (zs - 1)
+
     def lap(i, carry):
         @pl.when(i < npair)
         def _():
-            own_part(i)
+            g_copy(oth, i).wait_recv()
+
+        ahead = i - 1 - LAG * z
+
+        @pl.when((ahead >= 0) & (ahead < npair))
+        def _():
+            forward_part(ahead)
+
+        behind = i - 1 - LAG * (zs - 1 - z)
+
+        @pl.when((behind >= 0) & (behind < npair))
+        def _():
+            backward_part(behind)
+
+        @pl.when((i < npair - 1) & (i >= delay))
+        def _():
+            final_part(i - delay)
             local_part(i)
-
-        ahead = i - LAG * z
-
-        @pl.when((ahead >= 0) & (ahead < npair))
-        def _():
-            forward_part(ahead)
-
-        behind = i - LAG * (zs - 1 - z)
-
-        @pl.when((behind >= 0) & (behind < npair))
-        def _():
-            backward_part(behind)
-
-        @pl.when(i >= LAG * (zs - 1))
-        def _():
-            final_part(i - LAG * (zs - 1))
+            own_part(i + 1)
+
+        @pl.when((i < npair - 1) & (i < delay))
+        def _():
+            local_part(i)
+            own_part(i + 1)
+
+        @pl.when(i == npair - 1)
+        def _():
+            local_part(i)
+
+        @pl.when((i >= npair - 1) & (i >= delay))
+        def _():
+            final_part(i - delay)
 
         return carry
 
-    lax.fori_loop(0, npair + LAG * (zs - 1), lap, 0)
+    lax.fori_loop(0, npair + delay, lap, 0)
 
     def folded(a):
         return a[:, 0:tok] + a[:, tok:]
@@ -383,7 +399,7 @@
     for j in range(1, nhead):
         own_copy(lax.rem(hd + j, nhead), hd).start()
 
-    mine = ct[...] + cumul_of(par)
+    mine = ct[...] - ctf[...].T[0:heads] + cumul_of(par)
     lower = (t_sub >= t_lane).astype(F32)
     far_copy.wait_recv()
     decay_grad = lax.dot_general(
@@ -463,6 +479,17 @@
         gat_copy(lax.rem(hd + j, nhead), hd).wait_send()
     for j in range(1, nseq):
         hg_copy(lax.rem(me + j, nseq), me).wait_send()
+
+
+def publish(g_src, d_src, b_src, h_src, g_dst, d_dst, b_dst, h_dst, sems):
+    copies = [
+        pltpu.make_async_copy(src, dst, sems.at[i])
+        for i, (src, dst) in enumerate(((g_src, g_dst), (b_src, b_dst), (d_src, d_dst), (h_src, h_dst)))
+    ]
+    for copy in copies:
+        copy.start()
+    for copy in copies:
+        copy.wait()
 
 
 def local(
@@ -493,7 +520,7 @@
         vmem(npair, 4, *sq),
         vmem(npair, *sq), vmem(npair, *sq), vmem(npair, *sq), vmem(npair, *sq),
         vmem(*sq), vmem(tok, 2 * state), vmem(2, tok, 2 * state),
-        vmem(2, npair, tok), vmem(npair, tok), vmem(heads, tok),
+        vmem(2, npair, tok), vmem(npair, tok), vmem(heads, tok), vmem(*sq),
         vmem(2, *sq), vmem(1, *sq), vmem(heads, tok), vmem(heads, tok),
         vmem(nhead, 2, piece, state), vmem(nhead, piece, state),
         vmem(nhead, 2, piece, state), vmem(nhead, piece, state),
@@ -503,14 +530,15 @@
         dma(nseq), dma(nseq),
     ]
     whole = pl.BlockSpec(memory_space=pltpu.VMEM)
-    return tuple(pl.pallas_call(
+    shapes = (
+        jax.ShapeDtypeStruct((tok, channels), BF16),
+        jax.ShapeDtypeStruct((heads, tok), F32),
+        jax.ShapeDtypeStruct((2, tok, state), F32),
+        jax.ShapeDtypeStruct((2, heads), F32),
+    )
+    outs = pl.pallas_call(
         functools.partial(kernel, nseq, nhead, norm),
-        out_shape=(
-            jax.ShapeDtypeStruct((tok, channels), BF16),
-            jax.ShapeDtypeStruct((heads, tok), F32),
-            jax.ShapeDtypeStruct((2, tok, state), F32),
-            jax.ShapeDtypeStruct((2, heads), F32),
-        ),
+        out_shape=shapes,
         in_specs=[pl.BlockSpec(memory_space=pl.ANY)] * 6 + [whole] * 3 + [pl.BlockSpec(memory_space=pltpu.SMEM)],
         out_specs=(whole,) * 4,
         scratch_shapes=scratch,
@@ -520,7 +548,16 @@
     )(
         x_quant, scale_exp, dt_raw, b_proj, c_proj, grad_out, dt_bias.reshape(1, heads),
         a_log.reshape(1, heads), skip_weight.reshape(1, heads), doc_starts,
-    ))
+    )
+    anywhere = pl.BlockSpec(memory_space=pl.ANY)
+    return tuple(pl.pallas_call(
+        publish,
+        out_shape=shapes,
+        in_specs=[anywhere] * 4,
+        out_specs=(anywhere,) * 4,
+        scratch_shapes=[dma(4)],
+        compiler_params=pltpu.CompilerParams(vmem_limit_bytes=60 << 20),
+    )(*outs))
 
 
 def solution(mesh):

time: 63.6 us -> 78 us (1.23)
  Pallas kernels: 59 us -> 77.2 us
  local copies, waits for them, and re-layouts: 3.76 us -> 0 us
    pallas_call x1 -> x2, Pallas kernels: 59 us -> 77.2 us  [the longest x1 55.7 us: local(): pl.pallas_call(functools.partial(kernel, nseq, nhead, norm), out_shape=sh...]
    unnamed x10 -> x0, local copies, waits for them, and re-layouts: 3.76 us -> none
where the time goes in v5:
time: 78 us; the launch traced here: 77.8 us
  Pallas kernels  77.2 us (99%)
    pallas_call x1, Pallas kernels, local(): pl.pallas_call(functools.partial(kernel, nseq, nhead, norm), out_shape=sh...  55.7 us
    pallas_call x1, Pallas kernels, local(): pl.pallas_call(publish, out_shape=shapes, in_specs=[anywhere] * 4, out_sp...  21.5 us

profile of v5, /device:TPU:0, one launch (start us, length us, event | category | flops | bytes accessed | tf_op | source)
XLA Modules:
  0.0 77.8 jit_solution(11633861358602930924)
XLA Ops:
  0.6 55.7 %shard_map.129 = (bf16[128,2048]{1,0:T(8,128)(2,1)}, f32[32,128]{1,0:T(8,128)}, f32[2,128,128]{2,1,0:T(8,128)}, f32[2,32]{1,0:T(2,128)}) custom-call(bf16[128,2048]{1,0:T(8,128)(2,1)} %x_hbm.1, s32[16,128]{1,0:T(8,128)} %sc_hbm.1, bf16[32,128]{1,0:T(8,128)(2,1)} %dt_hbm.1, bf16[128,128]{1,0:T(8,128)(2,1)} %b_hbm.1, bf16[128,128]{1,0:T(8,128)(2,1)} %c_hbm.1, ...), custom_call_target="tpu_custom_call" | custom-call | tf_op jit(solution)/shard_map/pallas_call | solution.py:539
  56.3 21.5 %shard_map.130 = (bf16[128,2048]{1,0:T(8,128)(2,1)}, f32[32,128]{1,0:T(8,128)}, f32[2,128,128]{2,1,0:T(8,128)}, f32[2,32]{1,0:T(2,128)}) custom-call(bf16[128,2048]{1,0:T(8,128)(2,1)} %get-tuple-element.8.g_src, f32[32,128]{1,0:T(8,128)} %get-tuple-element.9.d_src, f32[2,128,128]{2,1,0:T(8,128)} %get-tuple-element.10.b_src, f32[2,32]{1,0:T(2,128)} %get-tuple-element.11.h_src), custom_call_target="tpu_custom_call" | custom-call | tf_op jit(solution)/shard_map/pallas_call | solution.py:553

commit v6 on v5

--- a/solution.py
+++ b/solution.py
@@ -9,7 +9,7 @@
 from jax.sharding import PartitionSpec as P
 
 HEAD_DIM = 64
-LAG = 3
+LAG = 4
 MESH = pl.DeviceIdType.MESH
 F32 = jnp.float32
 BF16 = jnp.bfloat16
@@ -46,7 +46,7 @@
     x_ref, sc_ref, dt_ref, b_ref, c_ref, g_ref,
     fac, steps, rates, skips, meta, cf, gg, xv, kern, same, first, last, cols,
     twice, turned, step_s, enter_s, exit_s, inner_s, xs_s, ge_s, loc, es, rs_, er, rr,
-    kg, bx, cx, ends, skp, ct, ctf, ctc, sgc, far, near, own_out, oth_out, red_own, red_oth, gat, hgp,
+    kg, bx, cx, ends, skp, ct, ctc, sgc, kg_b, kg_c, far, near, own_out, oth_out, red_own, red_oth, gat, hgp,
     in_sems, c_sems, meta_sems, g_send, g_recv, e_send, e_recv, r_send, r_recv, far_sems,
     own_send, own_recv, oth_send, oth_recv, gat_send, gat_recv, hg_send, hg_recv,
 ):
@@ -148,9 +148,6 @@
     kg[...] = jnp.zeros_like(kg)
     bx[...] = jnp.zeros_like(bx)
     cx[...] = jnp.zeros_like(cx)
-    ctc[...] = jnp.zeros_like(ctc)
-    ctf[...] = jnp.zeros_like(ctf)
-    sgc[...] = jnp.zeros_like(sgc)
 
     @pl.when(z == 0)
     def _():
@@ -194,6 +191,15 @@
 
     def decay_of(q, k):
         return enter_s[q, k, tok - 1:tok, :]
+
+    w_sub = lax.broadcasted_iota(jnp.int32, (8, 2 * tok), 0)
+    w_half = lax.div(lax.rem(lax.broadcasted_iota(jnp.int32, (8, 2 * tok), 1), tok), HEAD_DIM)
+    ones_half = (w_sub == w_half).astype(F32).astype(BF16)
+    ones_all = jnp.ones((8, 2 * tok), BF16)
+
+    def lane_sums(pattern, parts):
+        rows = jnp.concatenate([jnp.concatenate(split(part), axis=1) for part in parts], axis=0)
+        return mm(pattern, rows, ROWS)
 
     def own_part(k):
         factor = jnp.broadcast_to(fac[pl.ds(k, 1), :], (tok, tok)).T
@@ -228,12 +234,12 @@
             flow = part * kern_own
             flows.append(flow)
             total = part if total is None else total + part
-            ct[pl.ds(2 * k + i, 1), :] = jnp.sum(flow, axis=0, keepdims=True)
         kg[...] += total
-        kept = ctf[...]
+        across_t = lane_sums(ones_all, flows)
         for i in range(2):
-            kept = jnp.where(t_lane == 2 * k + i, jnp.sum(flows[i], axis=1, keepdims=True), kept)
-        ctf[...] = kept
+            ct[pl.ds(2 * k + i, 1), :] = (
+                jnp.sum(flows[i], axis=0, keepdims=True) - across_t[0:1, i * tok:(i + 1) * tok]
+            )
         inner_s[k] = mm(
             jnp.concatenate(highs + lows, axis=1), jnp.concatenate([g_two, g_two], axis=0), PLAIN
         )
@@ -289,16 +295,7 @@
             cx[q] += mm(wide(ge_s[q, k]), corner(high, low), ROWS)
             return (enter_s[q, k] * gg[q, k]) * read
 
-        def place(cols_ref, q, full):
-            kept = cols_ref[q]
-            for i in range(2):
-                part = jnp.where(lane_a if i == 0 else ~lane_a, full, 0.0)
-                part_sum = jnp.sum(part, axis=1, keepdims=True)
-                kept = kept + jnp.where(t_lane == 2 * k + i, part_sum, 0.0)
-            cols_ref[q] = kept
-
         through = entering(oth, entry_oth)
-        place(ctc, oth, through)
         ends[oth, pl.ds(k, 1), :] = jnp.sum(leave_oth * entry_oth, axis=0, keepdims=True) * decay_of(oth, k)
 
         x_val, g_val = xv[k], gg[par, k]
@@ -309,8 +306,13 @@
         back_w = exit_w * back
         input_total = inner_s[k] + back_w
         exit_terms = (step * x_val) * back_w
-        place(ctc, par, entering(par, entry_own) - exit_terms)
-        place(sgc, 0, input_total * x_val)
+        sums = lane_sums(ones_half, [
+            through, entering(par, entry_own) - exit_terms, input_total * x_val
+        ])
+        for i in range(2):
+            ctc[oth, pl.ds(2 * k + i, 1), :] = sums[i:i + 1, 0:tok]
+            ctc[par, pl.ds(2 * k + i, 1), :] = sums[i:i + 1, tok:2 * tok]
+            sgc[pl.ds(2 * k + i, 1), :] = sums[i:i + 1, 2 * tok:3 * tok]
         ends[par, pl.ds(k, 1), :] = (
             jnp.sum(exit_terms, axis=0, keepdims=True)
             + jnp.sum(leave_own * entry_own, axis=0, keepdims=True) * decay_of(par, k)
@@ -356,6 +358,8 @@
         @pl.when(i == npair - 1)
         def _():
             local_part(i)
+            kg_b[...] = mm2(kg[...], c_ref[...], PLAIN)
+            kg_c[...] = mm2(kg[...], b_ref[...], COLS)
 
         @pl.when((i >= npair - 1) & (i >= delay))
         def _():
@@ -388,18 +392,18 @@
     def cumul_of(q):
         per_head = jnp.broadcast_to(ends[q][:, None, :], (npair, 2, tok)).reshape(heads, tok)
         ending = jnp.sum(jnp.where(pick, per_head, 0.0), axis=1, keepdims=True)
-        return ctc[q].T[0:heads] + jnp.where(h_lane == tok - 1, ending, 0.0)
+        return ctc[q] + jnp.where(h_lane == tok - 1, ending, 0.0)
 
     far[...] = cumul_of(oth)
     far_copy = remote(far, near, far_sems.at[0], far_sems.at[1], across)
     far_copy.start()
 
-    own_out[:, 0] = (mm2(kg[...], c_ref[...], PLAIN) + folded(bx[...])).reshape(nhead, piece, state)
-    own_out[:, 1] = (mm2(kg[...], b_ref[...], COLS) + folded(cx[par])).reshape(nhead, piece, state)
+    own_out[:, 0] = (kg_b[...] + folded(bx[...])).reshape(nhead, piece, state)
+    own_out[:, 1] = (kg_c[...] + folded(cx[par])).reshape(nhead, piece, state)
     for j in range(1, nhead):
         own_copy(lax.rem(hd + j, nhead), hd).start()
 
-    mine = ct[...] - ctf[...].T[0:heads] + cumul_of(par)
+    mine = ct[...] + cumul_of(par)
     lower = (t_sub >= t_lane).astype(F32)
     far_copy.wait_recv()
     decay_grad = lax.dot_general(
@@ -443,7 +447,7 @@
         gat_copy(lax.rem(hd + j, nhead), hd).start()
 
     sigmoid = 1.0 / (1.0 + jnp.exp(-(dt_ref[...].astype(F32) + bias)))
-    dt_out[...] = (sgc[0].T[0:heads] - rates[...] * decay_grad) * sigmoid
+    dt_out[...] = (sgc[...] - rates[...] * decay_grad) * sigmoid
     for j in range(1, nseq):
         other = lax.rem(me + j, nseq)
         hg_copy(other, other).wait_recv()
@@ -481,14 +485,19 @@
         hg_copy(lax.rem(me + j, nseq), me).wait_send()
 
 
-def publish(g_src, d_src, b_src, h_src, g_dst, d_dst, b_dst, h_dst, sems):
-    copies = [
-        pltpu.make_async_copy(src, dst, sems.at[i])
-        for i, (src, dst) in enumerate(((g_src, g_dst), (b_src, b_dst), (d_src, d_dst), (h_src, h_dst)))
-    ]
-    for copy in copies:
+def publish(g_src, b_src, d_src, h_src, g_dst, b_dst, d_dst, h_dst, g_mid, b_mid, d_mid, h_mid, arrive, leave):
+    rows = g_src.shape[0] // 2
+    triples = [(g_src.at[pl.ds(i * rows, rows)], g_mid.at[pl.ds(i * rows, rows)], g_dst.at[pl.ds(i * rows, rows)])
+               for i in range(2)]
+    triples += [(b_src, b_mid, b_dst), (d_src, d_mid, d_dst), (h_src, h_mid, h_dst)]
+    first = [pltpu.make_async_copy(a, b, arrive.at[i]) for i, (a, b, c) in enumerate(triples)]
+    second = [pltpu.make_async_copy(b, c, leave.at[i]) for i, (a, b, c) in enumerate(triples)]
+    for copy in first:
         copy.start()
-    for copy in copies:
+    for one, two in zip(first, second):
+        one.wait()
+        two.start()
+    for copy in second:
         copy.wait()
 
 
@@ -520,8 +529,9 @@
         vmem(npair, 4, *sq),
         vmem(npair, *sq), vmem(npair, *sq), vmem(npair, *sq), vmem(npair, *sq),
         vmem(*sq), vmem(tok, 2 * state), vmem(2, tok, 2 * state),
-        vmem(2, npair, tok), vmem(npair, tok), vmem(heads, tok), vmem(*sq),
-        vmem(2, *sq), vmem(1, *sq), vmem(heads, tok), vmem(heads, tok),
+        vmem(2, npair, tok), vmem(npair, tok), vmem(heads, tok),
+        vmem(2, heads, tok), vmem(heads, tok), vmem(*sq), vmem(*sq),
+        vmem(heads, tok), vmem(heads, tok),
         vmem(nhead, 2, piece, state), vmem(nhead, piece, state),
         vmem(nhead, 2, piece, state), vmem(nhead, piece, state),
         vmem(nhead, 2, piece, state), vmem(nseq, 8, tok),
@@ -550,14 +560,16 @@
         a_log.reshape(1, heads), skip_weight.reshape(1, heads), doc_starts,
     )
     anywhere = pl.BlockSpec(memory_space=pl.ANY)
-    return tuple(pl.pallas_call(
+    order = (0, 2, 1, 3)
+    given = pl.pallas_call(
         publish,
-        out_shape=shapes,
+        out_shape=tuple(shapes[i] for i in order),
         in_specs=[anywhere] * 4,
         out_specs=(anywhere,) * 4,
-        scratch_shapes=[dma(4)],
+        scratch_shapes=[pltpu.VMEM(shapes[i].shape, shapes[i].dtype) for i in order] + [dma(5), dma(5)],
         compiler_params=pltpu.CompilerParams(vmem_limit_bytes=60 << 20),
-    )(*outs))
+    )(*(outs[i] for i in order))
+    return tuple(given[i] for i in order)
 
 
 def solution(mesh):

time: 78 us -> 61.2 us (0.78)
  Pallas kernels: 77.2 us -> 60.4 us
    pallas_call x1, Pallas kernels: 21.5 us -> 1.87 us  [local(): pl.pallas_call(publish, out_shape=tuple((shapes[i] for i in order)), in_s...]
    pallas_call x1, Pallas kernels: 55.7 us -> 58.5 us  [local(): pl.pallas_call(functools.partial(kernel, nseq, nhead, norm), out_shape=sh...]
where the time goes in v6:
time: 61.2 us; the launch traced here: 61 us
  Pallas kernels  60.4 us (99%)
  between operations  0.64 us (1%)
    pallas_call x1, Pallas kernels, local(): pl.pallas_call(functools.partial(kernel, nseq, nhead, norm), out_shape=sh...  58.5 us
    pallas_call x1, Pallas kernels, local(): pl.pallas_call(publish, out_shape=tuple((shapes[i] for i in order)), in_s...  1.87 us

profile of v6, /device:TPU:0, one launch (start us, length us, event | category | flops | bytes accessed | tf_op | source)
XLA Modules:
  0.0 61.0 jit_solution(1725601279374118677)
XLA Ops:
  0.6 58.5 %shard_map.129 = (bf16[128,2048]{1,0:T(8,128)(2,1)}, f32[32,128]{1,0:T(8,128)}, f32[2,128,128]{2,1,0:T(8,128)}, f32[2,32]{1,0:T(2,128)}) custom-call(bf16[128,2048]{1,0:T(8,128)(2,1)} %x_hbm.1, s32[16,128]{1,0:T(8,128)} %sc_hbm.1, bf16[32,128]{1,0:T(8,128)(2,1)} %dt_hbm.1, bf16[128,128]{1,0:T(8,128)(2,1)} %b_hbm.1, bf16[128,128]{1,0:T(8,128)(2,1)} %c_hbm.1, ...), custom_call_target="tpu_custom_call" | custom-call | tf_op jit(solution)/shard_map/pallas_call | solution.py:549
  59.2 1.9 %shard_map.130 = (bf16[128,2048]{1,0:T(8,128)(2,1)}, f32[2,128,128]{2,1,0:T(8,128)}, f32[32,128]{1,0:T(8,128)}, f32[2,32]{1,0:T(2,128)}) custom-call(bf16[128,2048]{1,0:T(8,128)(2,1)} %get-tuple-element.12.g_src, f32[2,128,128]{2,1,0:T(8,128)} %get-tuple-element.13.b_src, f32[32,128]{1,0:T(8,128)} %get-tuple-element.14.d_src, f32[2,32]{1,0:T(2,128)} %get-tuple-element.15.h_src), custom_call_target="tpu_custom_call" | custom-call | tf_op jit(solution)/shard_map/pallas_call | solution.py:564

commit v7 on v5

--- a/solution.py
+++ b/solution.py
@@ -46,7 +46,7 @@
     x_ref, sc_ref, dt_ref, b_ref, c_ref, g_ref,
     fac, steps, rates, skips, meta, cf, gg, xv, kern, same, first, last, cols,
     twice, turned, step_s, enter_s, exit_s, inner_s, xs_s, ge_s, loc, es, rs_, er, rr,
-    kg, bx, cx, ends, skp, ct, ctf, ctc, sgc, far, near, own_out, oth_out, red_own, red_oth, gat, hgp,
+    kg, bx, cx, ends, skp, ct, ctf, ctc, sgc, kg_b, kg_c, far, near, own_out, oth_out, red_own, red_oth, gat, hgp,
     in_sems, c_sems, meta_sems, g_send, g_recv, e_send, e_recv, r_send, r_recv, far_sems,
     own_send, own_recv, oth_send, oth_recv, gat_send, gat_recv, hg_send, hg_recv,
 ):
@@ -270,10 +270,10 @@
     def wide(a):
         return jnp.concatenate([a[0:tok], a[tok:2 * tok]], axis=1)
 
-    def corner(high, low):
-        return jnp.concatenate(
-            [jnp.concatenate([high, high], axis=1), jnp.concatenate([low, low], axis=1)], axis=0
-        )
+    def corner(state):
+        high, low = split(state.T)
+        both = jnp.concatenate([high, low], axis=1)
+        return jnp.concatenate([both, both], axis=0)
 
     def final_part(k):
         entry0, exit1 = er[k], rr[k]
@@ -286,7 +286,7 @@
         def entering(q, entry):
             high, low = split(entry)
             read = mm(twice[q], jnp.concatenate([high, low], axis=0), PLAIN)
-            cx[q] += mm(wide(ge_s[q, k]), corner(high, low), ROWS)
+            cx[q] += mm(wide(ge_s[q, k]), corner(entry), PLAIN)
             return (enter_s[q, k] * gg[q, k]) * read
 
         def place(cols_ref, q, full):
@@ -305,7 +305,7 @@
         exit_w, step = exit_s[k], step_s[k]
         l_high, l_low = split(leave_own)
         back = mm(twice[2], jnp.concatenate([l_high, l_low], axis=0), PLAIN)
-        bx[...] += mm(wide(xs_s[k]), corner(l_high, l_low), ROWS)
+        bx[...] += mm(wide(xs_s[k]), corner(leave_own), PLAIN)
         back_w = exit_w * back
         input_total = inner_s[k] + back_w
         exit_terms = (step * x_val) * back_w
@@ -356,6 +356,8 @@
         @pl.when(i == npair - 1)
         def _():
             local_part(i)
+            kg_b[...] = mm2(kg[...], c_ref[...], PLAIN)
+            kg_c[...] = mm2(kg[...], b_ref[...], COLS)
 
         @pl.when((i >= npair - 1) & (i >= delay))
         def _():
@@ -394,8 +396,8 @@
     far_copy = remote(far, near, far_sems.at[0], far_sems.at[1], across)
     far_copy.start()
 
-    own_out[:, 0] = (mm2(kg[...], c_ref[...], PLAIN) + folded(bx[...])).reshape(nhead, piece, state)
-    own_out[:, 1] = (mm2(kg[...], b_ref[...], COLS) + folded(cx[par])).reshape(nhead, piece, state)
+    own_out[:, 0] = (kg_b[...] + folded(bx[...])).reshape(nhead, piece, state)
+    own_out[:, 1] = (kg_c[...] + folded(cx[par])).reshape(nhead, piece, state)
     for j in range(1, nhead):
         own_copy(lax.rem(hd + j, nhead), hd).start()
 
@@ -481,14 +483,19 @@
         hg_copy(lax.rem(me + j, nseq), me).wait_send()
 
 
-def publish(g_src, d_src, b_src, h_src, g_dst, d_dst, b_dst, h_dst, sems):
-    copies = [
-        pltpu.make_async_copy(src, dst, sems.at[i])
-        for i, (src, dst) in enumerate(((g_src, g_dst), (b_src, b_dst), (d_src, d_dst), (h_src, h_dst)))
-    ]
-    for copy in copies:
+def publish(g_src, b_src, d_src, h_src, g_dst, b_dst, d_dst, h_dst, g_mid, b_mid, d_mid, h_mid, arrive, leave):
+    rows = g_src.shape[0] // 2
+    triples = [(g_src.at[pl.ds(i * rows, rows)], g_mid.at[pl.ds(i * rows, rows)], g_dst.at[pl.ds(i * rows, rows)])
+               for i in range(2)]
+    triples += [(b_src, b_mid, b_dst), (d_src, d_mid, d_dst), (h_src, h_mid, h_dst)]
+    first = [pltpu.make_async_copy(a, b, arrive.at[i]) for i, (a, b, c) in enumerate(triples)]
+    second = [pltpu.make_async_copy(b, c, leave.at[i]) for i, (a, b, c) in enumerate(triples)]
+    for copy in first:
         copy.start()
-    for copy in copies:
+    for one, two in zip(first, second):
+        one.wait()
+        two.start()
+    for copy in second:
         copy.wait()
 
 
@@ -521,7 +528,8 @@
         vmem(npair, *sq), vmem(npair, *sq), vmem(npair, *sq), vmem(npair, *sq),
         vmem(*sq), vmem(tok, 2 * state), vmem(2, tok, 2 * state),
         vmem(2, npair, tok), vmem(npair, tok), vmem(heads, tok), vmem(*sq),
-        vmem(2, *sq), vmem(1, *sq), vmem(heads, tok), vmem(heads, tok),
+        vmem(2, *sq), vmem(1, *sq), vmem(*sq), vmem(*sq),
+        vmem(heads, tok), vmem(heads, tok),
         vmem(nhead, 2, piece, state), vmem(nhead, piece, state),
         vmem(nhead, 2, piece, state), vmem(nhead, piece, state),
         vmem(nhead, 2, piece, state), vmem(nseq, 8, tok),
@@ -550,14 +558,16 @@
         a_log.reshape(1, heads), skip_weight.reshape(1, heads), doc_starts,
     )
     anywhere = pl.BlockSpec(memory_space=pl.ANY)
-    return tuple(pl.pallas_call(
+    order = (0, 2, 1, 3)
+    given = pl.pallas_call(
         publish,
-        out_shape=shapes,
+        out_shape=tuple(shapes[i] for i in order),
         in_specs=[anywhere] * 4,
         out_specs=(anywhere,) * 4,
-        scratch_shapes=[dma(4)],
+        scratch_shapes=[pltpu.VMEM(shapes[i].shape, shapes[i].dtype) for i in order] + [dma(5), dma(5)],
         compiler_params=pltpu.CompilerParams(vmem_limit_bytes=60 << 20),
-    )(*outs))
+    )(*(outs[i] for i in order))
+    return tuple(given[i] for i in order)
 
 
 def solution(mesh):

time: 78 us -> 58.4 us (0.75)
  Pallas kernels: 77.2 us -> 57.6 us
    pallas_call x1, Pallas kernels: 21.5 us -> 1.87 us  [local(): pl.pallas_call(publish, out_shape=tuple((shapes[i] for i in order)), in_s...]
where the time goes in v7:
time: 58.4 us; the launch traced here: 58.3 us
  Pallas kernels  57.6 us (99%)
  between operations  0.64 us (1%)
    pallas_call x1, Pallas kernels, local(): pl.pallas_call(functools.partial(kernel, nseq, nhead, norm), out_shape=sh...  55.8 us
    pallas_call x1, Pallas kernels, local(): pl.pallas_call(publish, out_shape=tuple((shapes[i] for i in order)), in_s...  1.87 us

profile of v7, /device:TPU:0, one launch (start us, length us, event | category | flops | bytes accessed | tf_op | source)
XLA Modules:
  0.0 58.3 jit_solution(14385980766804231991)
XLA Ops:
  0.6 55.8 %shard_map.129 = (bf16[128,2048]{1,0:T(8,128)(2,1)}, f32[32,128]{1,0:T(8,128)}, f32[2,128,128]{2,1,0:T(8,128)}, f32[2,32]{1,0:T(2,128)}) custom-call(bf16[128,2048]{1,0:T(8,128)(2,1)} %x_hbm.1, s32[16,128]{1,0:T(8,128)} %sc_hbm.1, bf16[32,128]{1,0:T(8,128)(2,1)} %dt_hbm.1, bf16[128,128]{1,0:T(8,128)(2,1)} %b_hbm.1, bf16[128,128]{1,0:T(8,128)(2,1)} %c_hbm.1, ...), custom_call_target="tpu_custom_call" | custom-call | tf_op jit(solution)/shard_map/pallas_call | solution.py:547
  56.4 1.9 %shard_map.130 = (bf16[128,2048]{1,0:T(8,128)(2,1)}, f32[2,128,128]{2,1,0:T(8,128)}, f32[32,128]{1,0:T(8,128)}, f32[2,32]{1,0:T(2,128)}) custom-call(bf16[128,2048]{1,0:T(8,128)(2,1)} %get-tuple-element.12.g_src, f32[2,128,128]{2,1,0:T(8,128)} %get-tuple-element.13.b_src, f32[32,128]{1,0:T(8,128)} %get-tuple-element.14.d_src, f32[2,32]{1,0:T(2,128)} %get-tuple-element.15.h_src), custom_call_target="tpu_custom_call" | custom-call | tf_op jit(solution)/shard_map/pallas_call | solution.py:562

commit v8 on v7

--- a/solution.py
+++ b/solution.py
@@ -9,7 +9,7 @@
 from jax.sharding import PartitionSpec as P
 
 HEAD_DIM = 64
-LAG = 3
+LAG = 2
 MESH = pl.DeviceIdType.MESH
 F32 = jnp.float32
 BF16 = jnp.bfloat16

time: 58.4 us -> 62.6 us (1.072)
  Pallas kernels: 57.6 us -> 61.8 us
    pallas_call x1, Pallas kernels: 55.8 us -> 59.9 us  [local(): pl.pallas_call(functools.partial(kernel, nseq, nhead, norm), out_shape=sh...]
where the time goes in v8:
time: 62.6 us; the launch traced here: 62.4 us
  Pallas kernels  61.8 us (99%)
  between operations  0.64 us (1%)
    pallas_call x1, Pallas kernels, local(): pl.pallas_call(functools.partial(kernel, nseq, nhead, norm), out_shape=sh...  59.9 us
    pallas_call x1, Pallas kernels, local(): pl.pallas_call(publish, out_shape=tuple((shapes[i] for i in order)), in_s...  1.87 us

profile of v8, /device:TPU:0, one launch (start us, length us, event | category | flops | bytes accessed | tf_op | source)
XLA Modules:
  0.0 62.4 jit_solution(7502456112511330791)
XLA Ops:
  0.6 59.9 %shard_map.129 = (bf16[128,2048]{1,0:T(8,128)(2,1)}, f32[32,128]{1,0:T(8,128)}, f32[2,128,128]{2,1,0:T(8,128)}, f32[2,32]{1,0:T(2,128)}) custom-call(bf16[128,2048]{1,0:T(8,128)(2,1)} %x_hbm.1, s32[16,128]{1,0:T(8,128)} %sc_hbm.1, bf16[32,128]{1,0:T(8,128)(2,1)} %dt_hbm.1, bf16[128,128]{1,0:T(8,128)(2,1)} %b_hbm.1, bf16[128,128]{1,0:T(8,128)(2,1)} %c_hbm.1, ...), custom_call_target="tpu_custom_call" | custom-call | tf_op jit(solution)/shard_map/pallas_call | solution.py:547
  60.5 1.9 %shard_map.130 = (bf16[128,2048]{1,0:T(8,128)(2,1)}, f32[2,128,128]{2,1,0:T(8,128)}, f32[32,128]{1,0:T(8,128)}, f32[2,32]{1,0:T(2,128)}) custom-call(bf16[128,2048]{1,0:T(8,128)(2,1)} %get-tuple-element.12.g_src, f32[2,128,128]{2,1,0:T(8,128)} %get-tuple-element.13.b_src, f32[32,128]{1,0:T(8,128)} %get-tuple-element.14.d_src, f32[2,32]{1,0:T(2,128)} %get-tuple-element.15.h_src), custom_call_target="tpu_custom_call" | custom-call | tf_op jit(solution)/shard_map/pallas_call | solution.py:562
